TPU v7x, 32 devices: a whole 2x2x4 slice. The times are simulated.
32 devices in a mesh: dp: 8 (over z, y), ctx: 4 (over x, core).
Axes of the slice: x: 2, y: 2, z: 4, core: 2. Of those that a mesh axis runs over, the one named last changes fastest.
Arguments:
- tokens: bfloat16 [2, 4096, 1088], P(None, ('dp', 'ctx')), may hold values from -6 to 6
- cotangent: bfloat16 [2, 4096, 1088], P(None, ('dp', 'ctx')), may hold values from -6 to 6
- w_attn: bfloat16 [1088, 4352], P(None, ('dp', 'ctx'))
- w_up: bfloat16 [1088, 4352], P(None, ('dp', 'ctx')), may hold values from -0.1875 to 0.1875
- w_down: bfloat16 [4352, 1088], P(('dp', 'ctx')), may hold values from -0.09375 to 0.09375
- vectors: bfloat16 [13056], P(('dp', 'ctx'))
- segments: int32 [2, 8, 512], P(None, 'dp'), may hold values from 0 to 511, as said below
Outputs:
- mixed: bfloat16 [2, 4096, 1088], P(None, ('dp', 'ctx'))
- input_grad: bfloat16 [2, 4096, 1088], P(None, ('dp', 'ctx'))
- attn_grad: float32 [1088, 4352], P(None, ('dp', 'ctx'))
- up_grad: float32 [1088, 4352], P(None, ('dp', 'ctx'))
- down_grad: float32 [4352, 1088], P(('dp', 'ctx'))
- vector_grad: float32 [13056], P(('dp', 'ctx'))
Inputs may be any that keep to these rules, and one draw needn't show every extreme that they name: `segments`: entries never fall along a group's rows; each equals the row where its sequence starts (the first row of a group starts one; a sequence may be a single row). In every group and micro-batch one sequence has rows on the first and the last of the group's ctx devices.
All inputs are finite; a program needn't handle non-finite values.
Results may differ from a plain program's by a relative error of at most 0.014.
Values may be sent and summed in bfloat16 or wider, within the bound.
No kernel may reach another device: no remote copies, remote signals or barrier semaphores. Data moves between devices by JAX's collectives and lax.ppermute only.
A program may use at most 256 MiB of HBM per device.

v0:
```python
from functools import partial

import jax
import jax.numpy as jnp
from jax import lax
from jax.sharding import PartitionSpec as P

HEAD_DIM = 64


NEG_FILL = -1e30
EPSILON = 1e-05


def norm_rows(values, gain_vec, bias_vec):
    row_mean = jnp.mean(values, axis=-1, keepdims=True)
    centred = values - row_mean
    variance = jnp.mean(centred * centred, axis=-1, keepdims=True)
    return centred * lax.rsqrt(variance + EPSILON) * gain_vec + bias_vec


def split_vectors(vectors, model_width):
    pieces = [vectors[member * model_width : (member + 1) * model_width] for member in range(8)]
    return pieces + [vectors[8 * model_width :]]


def contract_rows(left, right):
    return lax.dot_general(
        left, right, (((0,), (0,)), ((), ())), preferred_element_type=jnp.float32
    )


def contract_cols(left, right):
    return lax.dot_general(
        left, right, (((1,), (1,)), ((), ())), preferred_element_type=jnp.float32
    )


def score_block(queries, arriving, starts, query_pos, seg_query):
    row_count, head_count, head_dim = queries.shape
    model_width = head_count * head_dim
    key_count = arriving.shape[0]
    key_part = arriving[:, :model_width].reshape(key_count, head_count, head_dim)
    value_part = arriving[:, model_width:].reshape(key_count, head_count, head_dim)
    scores = jnp.einsum(
        "qhd,khd->hqk", queries, key_part, preferred_element_type=jnp.float32
    ) * head_dim ** (-0.5)
    key_pos = jnp.arange(key_count, dtype=jnp.int32)
    allowed = (key_pos[None, :] <= query_pos[:, None]) & (starts[None, :] == seg_query[:, None])
    return (jnp.where(allowed[None], scores, NEG_FILL), allowed, key_part, value_part)


def attend_forward(queries, key_values, starts, query_pos, seg_query):
    row_count, head_count, head_dim = queries.shape

    def absorb(running, arriving, first_row):
        row_top, total, accum = running
        scores, allowed, key_part, value_part = score_block(
            queries, arriving, starts, query_pos, seg_query
        )
        new_top = jnp.maximum(row_top, jnp.max(scores, axis=-1))
        weights = jnp.where(allowed[None], jnp.exp(scores - new_top[:, :, None]), 0.0)
        fading = jnp.exp(row_top - new_top)
        total = jnp.sum(weights, axis=-1)
        accum = accum * fading.T[:, :, None] + jnp.einsum(
            "hqk,khd->qhd",
            weights.astype(jnp.bfloat16),
            value_part,
            preferred_element_type=jnp.float32,
        )
        return (new_top, total, accum)

    initial = (
        jnp.full((head_count, row_count), NEG_FILL, jnp.float32),
        jnp.zeros((head_count, row_count), jnp.float32),
        jnp.zeros((row_count, head_count, head_dim), jnp.float32),
    )
    row_top, total, accum = absorb(
        initial, lax.all_gather(key_values, "ctx", axis=0, tiled=True), jnp.int32(0)
    )
    attended = accum / total.T[:, :, None]
    return (attended, row_top + jnp.log(total))


def attend_backward(
    queries, key_values, grad_heads, log_total, delta, starts, query_pos, seg_query, group_rows
):
    row_count, head_count, head_dim = queries.shape
    model_width = head_count * head_dim
    scale = head_dim ** (-0.5)

    def absorb(running, arriving, first_row):
        key_count = arriving.shape[0]
        scores, allowed, key_part, value_part = score_block(
            queries, arriving, starts, query_pos, seg_query
        )
        probs = jnp.where(allowed[None], jnp.exp(scores - log_total[:, :, None]), 0.0)
        grad_probs = jnp.einsum(
            "qhd,khd->hqk", grad_heads, value_part, preferred_element_type=jnp.float32
        )
        grad_scores = (probs * (grad_probs - delta[:, :, None])).astype(jnp.bfloat16)
        grad_queries = scale * jnp.einsum(
            "hqk,khd->qhd", grad_scores, key_part, preferred_element_type=jnp.float32
        )
        key_grad = scale * jnp.einsum(
            "hqk,qhd->khd", grad_scores, queries, preferred_element_type=jnp.float32
        )
        value_grad = jnp.einsum(
            "hqk,qhd->khd",
            probs.astype(jnp.bfloat16),
            grad_heads,
            preferred_element_type=jnp.float32,
        )
        update = jnp.concatenate(
            [key_grad.reshape(key_count, model_width), value_grad.reshape(key_count, model_width)],
            axis=1,
        )
        return (grad_queries, update)

    initial = (
        jnp.zeros((row_count, head_count, head_dim), jnp.float32),
        jnp.zeros((group_rows, 2 * model_width), jnp.float32),
    )
    grad_queries, grad_keys = absorb(
        initial, lax.all_gather(key_values, "ctx", axis=0, tiled=True), jnp.int32(0)
    )
    grad_kv = lax.psum_scatter(
        grad_keys.astype(jnp.bfloat16), "ctx", scatter_dimension=0, tiled=True
    ).astype(jnp.float32)
    return (grad_queries, grad_kv)


def forward_layer(block_in, weights, starts, query_pos, seg_query):
    w_attn, w_up, w_down, vectors = weights
    row_count, model_width = block_in.shape
    head_count = model_width // HEAD_DIM
    pieces = split_vectors(vectors.astype(jnp.float32), model_width)
    gain_one, bias_one, q_bias, v_bias, out_bias, gain_two, bias_two, down_bias, up_bias = pieces
    inputs32 = block_in.astype(jnp.float32)
    normed_one = norm_rows(inputs32, gain_one, bias_one).astype(jnp.bfloat16)
    qkv_bias = jnp.concatenate([q_bias, jnp.zeros_like(q_bias), v_bias])
    projected = (
        jnp.dot(normed_one, w_attn[:, : 3 * model_width], preferred_element_type=jnp.float32)
        + qkv_bias
    ).astype(jnp.bfloat16)
    queries = projected[:, :model_width].reshape(row_count, head_count, HEAD_DIM)
    key_values = projected[:, model_width:]
    attended, log_total = attend_forward(queries, key_values, starts, query_pos, seg_query)
    heads_out = attended.reshape(row_count, model_width).astype(jnp.bfloat16)
    middle = inputs32 + contract_cols(heads_out, w_attn[:, 3 * model_width :]) + out_bias
    normed_two = norm_rows(middle, gain_two, bias_two).astype(jnp.bfloat16)
    hidden_pre = jnp.dot(normed_two, w_up, preferred_element_type=jnp.float32) + up_bias
    active = jax.nn.gelu(hidden_pre, approximate=True).astype(jnp.bfloat16)
    block_out = middle + jnp.dot(active, w_down, preferred_element_type=jnp.float32) + down_bias
    saved = (
        inputs32,
        normed_one,
        queries,
        key_values,
        attended,
        log_total,
        heads_out,
        middle,
        normed_two,
        hidden_pre,
        active,
    )
    return (block_out.astype(jnp.bfloat16), saved)


def backward_layer(grad_in, weights, saved, starts, query_pos, seg_query, group_rows):
    w_attn, w_up, w_down, vectors = weights
    (
        inputs32,
        normed_one,
        queries,
        key_values,
        attended,
        log_total,
        heads_out,
        middle,
        normed_two,
        hidden_pre,
        active,
    ) = saved
    row_count, model_width = inputs32.shape
    head_count = model_width // HEAD_DIM
    pieces = split_vectors(vectors.astype(jnp.float32), model_width)
    gain_one, bias_one, gain_two, bias_two = (pieces[0], pieces[1], pieces[5], pieces[6])
    grad_out = grad_in.astype(jnp.float32)
    grad_down = contract_rows(active, grad_in)
    down_bias_grad = jnp.sum(grad_out, axis=0)
    grad_active = contract_cols(grad_in, w_down)
    gelu_pull = jax.vjp(partial(jax.nn.gelu, approximate=True), hidden_pre)[1]
    grad_hidden = gelu_pull(grad_active)[0].astype(jnp.bfloat16)
    grad_up_turned = contract_rows(grad_hidden, normed_two)
    up_bias_grad = jnp.sum(grad_hidden.astype(jnp.float32), axis=0)
    grad_normed_two = contract_cols(grad_hidden, w_up)
    pull_two = jax.vjp(norm_rows, middle, gain_two, bias_two)[1]
    grad_middle_part, gain_two_grad, bias_two_grad = pull_two(grad_normed_two)
    grad_middle = grad_out + grad_middle_part
    grad_branch = grad_middle.astype(jnp.bfloat16)
    out_bias_grad = jnp.sum(grad_branch.astype(jnp.float32), axis=0)
    grad_out_turned = contract_rows(heads_out, grad_branch)
    grad_heads = jnp.dot(
        grad_branch, w_attn[:, 3 * model_width :], preferred_element_type=jnp.float32
    )
    grad_heads = grad_heads.astype(jnp.bfloat16).reshape(row_count, head_count, HEAD_DIM)
    delta = jnp.einsum("qhd,qhd->hq", grad_heads.astype(jnp.float32), attended)
    grad_queries, grad_kv = attend_backward(
        queries, key_values, grad_heads, log_total, delta, starts, query_pos, seg_query, group_rows
    )
    grad_proj = jnp.concatenate(
        [grad_queries.reshape(row_count, model_width), grad_kv], axis=1
    ).astype(jnp.bfloat16)
    grad_qkv_turned = contract_rows(grad_proj, normed_one)
    proj_bias_grad = jnp.sum(grad_proj.astype(jnp.float32), axis=0)
    grad_normed_one = contract_cols(grad_proj, w_attn[:, : 3 * model_width])
    pull_one = jax.vjp(norm_rows, inputs32, gain_one, bias_one)[1]
    grad_inputs_part, gain_one_grad, bias_one_grad = pull_one(grad_normed_one)
    grad_inputs = (grad_middle + grad_inputs_part).astype(jnp.bfloat16)
    attn_turned = jnp.concatenate([grad_qkv_turned, grad_out_turned], axis=0)
    vector_part = jnp.concatenate(
        [
            gain_one_grad,
            bias_one_grad,
            proj_bias_grad[:model_width],
            proj_bias_grad[2 * model_width :],
            out_bias_grad,
            gain_two_grad,
            bias_two_grad,
            down_bias_grad,
            up_bias_grad,
        ]
    )
    return (grad_inputs, (attn_turned, grad_up_turned, grad_down, vector_part))


def shards(tokens, cotangent, w_attn, w_up, w_down, vectors, segments):
    micro_count, row_count, model_width = tokens.shape
    device_count = lax.axis_size(("dp", "ctx"))
    group_rows = row_count * lax.axis_size("ctx")
    ctx_rank = lax.axis_index("ctx")
    query_pos = ctx_rank * row_count + jnp.arange(row_count, dtype=jnp.int32)
    hidden_units = w_up.shape[1] * device_count
    accum_attn = jnp.zeros((4 * model_width, model_width), jnp.float32)
    accum_up = jnp.zeros((hidden_units, model_width), jnp.float32)
    accum_down = jnp.zeros((hidden_units, model_width), jnp.float32)
    accum_vec = jnp.zeros((vectors.shape[0] * device_count,), jnp.float32)
    outputs = []
    input_grads = []
    for micro_step in range(micro_count):
        forward_weights = (
            lax.all_gather(w_attn, ("dp", "ctx"), axis=1, tiled=True),
            lax.all_gather(w_up, ("dp", "ctx"), axis=1, tiled=True),
            lax.all_gather(w_down, ("dp", "ctx"), axis=0, tiled=True),
            lax.all_gather(vectors, ("dp", "ctx"), axis=0, tiled=True),
        )
        starts = segments[micro_step, 0]
        seg_query = lax.dynamic_slice_in_dim(starts, ctx_rank * row_count, row_count)
        block_out, saved = forward_layer(
            tokens[micro_step], forward_weights, starts, query_pos, seg_query
        )
        outputs.append(block_out)
        backward_weights = (
            lax.all_gather(w_attn, ("dp", "ctx"), axis=1, tiled=True),
            lax.all_gather(w_up, ("dp", "ctx"), axis=1, tiled=True),
            lax.all_gather(w_down, ("dp", "ctx"), axis=0, tiled=True),
            lax.all_gather(vectors, ("dp", "ctx"), axis=0, tiled=True),
        )
        grad_inputs, terms = backward_layer(
            cotangent[micro_step], backward_weights, saved, starts, query_pos, seg_query, group_rows
        )
        input_grads.append(grad_inputs)
        accum_attn = accum_attn + terms[0]
        accum_up = accum_up + terms[1]
        accum_down = accum_down + terms[2]
        accum_vec = accum_vec + terms[3]
    owned = (
        lax.psum_scatter(accum_attn, ("dp", "ctx"), scatter_dimension=0, tiled=True),
        lax.psum_scatter(accum_up, ("dp", "ctx"), scatter_dimension=0, tiled=True),
        lax.psum_scatter(accum_down, ("dp", "ctx"), scatter_dimension=0, tiled=True),
        lax.psum_scatter(accum_vec, ("dp", "ctx"), scatter_dimension=0, tiled=True),
    )
    return (jnp.stack(outputs), jnp.stack(input_grads), owned[0].T, owned[1].T, owned[2], owned[3])


def solution(mesh):
    return jax.shard_map(
        shards,
        mesh=mesh,
        in_specs=(
            P(None, ("dp", "ctx"), None),
            P(None, ("dp", "ctx"), None),
            P(None, ("dp", "ctx")),
            P(None, ("dp", "ctx")),
            P(("dp", "ctx"), None),
            P(("dp", "ctx")),
            P(None, "dp", None),
        ),
        out_specs=(
            P(None, ("dp", "ctx"), None),
            P(None, ("dp", "ctx"), None),
            P(None, ("dp", "ctx")),
            P(None, ("dp", "ctx")),
            P(("dp", "ctx"), None),
            P(("dp", "ctx")),
        ),
        check_vma=False,
    )
```

profile of v0, /device:TPU:0, one launch (start us, length us, event | category | flops | bytes accessed | tf_op | source)
XLA Modules:
  0.0 1220.7 jit_solution(4246411264638971336)
XLA Ops:
  8.8 42.9 %all-reduce = bf16[13056]{0:T(1024)(128)(2,1)S(1)} all-reduce(bf16[13056]{0:T(1024)(128)(2,1)S(1)} %dynamic-update-slice), channel_id=1, replica_groups=mesh['dp'=8,'ctx'=4] {'dp','ctx'}, use_global_device_ids=true, to_apply=%add | all-reduce | flops 13056 | bytes 52224
  55.0 44.1 %all-gather.6.cloned.1.call-done = bf16[1088,4352]{0,1:T(8,128)(2,1)} async-done(((bf16[1088,136]{0,1:T(8,128)(2,1)}), bf16[1088,4352]{0,1:T(8,128)(2,1)}) %all-gather.6.cloned.1.call-update) | async-done | bytes 9469968 | tf_op jit(solution)/shard_map/all_gather | solution.py:254
  114.0 13.8 %all-gather.8.cloned.1.call-done = bf16[512,2176]{0,1:T(8,128)(2,1)} async-done(((bf16[128,2176]{0,1:T(8,128)(2,1)}), bf16[512,2176]{0,1:T(8,128)(2,1)}) %all-gather.8.cloned.1.call-update) | async-done | bytes 2228240 | tf_op jit(solution)/shard_map/all_gather | solution.py:79
  138.3 15.3 %all-gather.14.cloned.1.call-done = bf16[512,2176]{0,1:T(8,128)(2,1)} async-done(((bf16[128,2176]{0,1:T(8,128)(2,1)}), bf16[512,2176]{0,1:T(8,128)(2,1)}) %all-gather.14.cloned.1.call-update) | async-done | bytes 2228240 | tf_op jit(solution)/shard_map/all_gather | solution.py:79
  163.8 77.3 %all-gather.10.cloned.1.call-done = bf16[1088,4352]{0,1:T(8,128)(2,1)} async-done(((bf16[1088,136]{0,1:T(8,128)(2,1)}), bf16[1088,4352]{0,1:T(8,128)(2,1)}) %all-gather.10.cloned.1.call-update) | async-done | bytes 9469968 | tf_op jit(solution)/shard_map/all_gather | solution.py:255
  241.1 8.8 convolution_add_fusion.3
  254.4 72.8 %all-gather.12.cloned.1.call-done = bf16[4352,1088]{1,0:T(8,128)(2,1)} async-done(((bf16[136,1088]{1,0:T(8,128)(2,1)}), bf16[4352,1088]{1,0:T(8,128)(2,1)}) %all-gather.12.cloned.1.call-update) | async-done | bytes 9469968 | tf_op jit(solution)/shard_map/all_gather | solution.py:256
  327.2 8.3 convert_reduce_fusion.1
  335.5 8.0 convert_reduce_fusion
  393.4 6.0 reduce-scatter.16.cloned.1.call-done
  401.6 9.2 fusion.135
  410.8 23.8 %reduce-scatter.14.cloned.1.call-done = bf16[128,2176]{1,0:T(8,128)(2,1)} async-done(((bf16[512,2176]{1,0:T(8,128)(2,1)}), bf16[128,2176]{1,0:T(8,128)(2,1)}) %reduce-scatter.14.cloned.1.call-update) | async-done | bytes 557072
  436.7 9.3 fusion.136
  446.0 18.9 %maximum_add_fusion = f32[4352,1088]{0,1:T(8,128)} fusion(f32[1088,1088]{0,1:T(8,128)} %fusion.183, f32[3264,1088]{0,1:T(8,128)} %fusion.136, f32[1088,1088]{0,1:T(8,128)} %fusion.184, f32[3264,1088]{0,1:T(8,128)S(1)} %copy-done.1), kind=kLoop, calls=%fused_computation.2 | loop fusion | flops 14204928 | bytes 56819712 | tf_op jit(solution)/shard_map/add | solution.py:275
  465.2 12.6 %fusion.127 = f32[4352,1088]{1,0:T(8,128)} fusion(bf16[2,128,1088]{1,2,0:T(8,128)(2,1)} %param.8, f32[128,4352]{1,0:T(8,128)} %convolution_add_fusion.3), kind=kOutput, calls=%fused_computation.169 | convolution fusion | flops 1217167360 | bytes 21446656 | tf_op jit(solution)/shard_map/dot_general | solution.py:28
  477.8 13.4 %convolution_add_fusion = f32[4352,1088]{1,0:T(8,128)} fusion(f32[4352,1088]{1,0:T(8,128)} %fusion.127, bf16[2,128,1088]{1,2,0:T(8,128)(2,1)S(1)} %copy-done.25, f32[128,4352]{1,0:T(8,128)S(1)} %convolution_add_fusion.2), kind=kOutput, calls=%fused_computation | convolution fusion | flops 1221902336 | bytes 40386560 | tf_op jit(solution)/shard_map/dot_general | solution.py:28
  491.8 11.2 fusion.167
  503.0 18.3 %convolution_add_fusion.1 = f32[4352,1088]{1,0:T(8,128)} fusion(f32[4352,1088]{1,0:T(8,128)} %fusion.167, bf16[128,4352]{1,0:T(8,128)(2,1)S(1)} %copy-done.17, f32[128,1088]{0,1:T(8,128)S(1)} %copy-done.8, f32[128]{0:T(128)S(1)} %copy-done.61, f32[128]{0:T(128)S(1)} %copy-done.54, f32[1088]{0:T(1024)S(1)} %get-tuple-element.59, f32[1088]{0:T(1024)S(1)} %get-tuple-element.58), kind=kOutput, calls=%fused_computation.1 | convolution fusion | flops 1217585152 | bytes 39560704 | tf_op jit(solution)/shard_map/dot_general | solution.py:28
  522.0 8.5 fusion.27
  530.6 8.1 fusion.26
  547.8 40.9 %all-reduce.4 = f32[13056]{0:T(1024)S(1)} all-reduce(f32[13056]{0:T(1024)S(1)} %add.272), channel_id=7, replica_groups=mesh['dp'=8,'ctx'=4] {'dp','ctx'}, use_global_device_ids=true, to_apply=%region_41.42.clone | all-reduce | flops 13056 | bytes 104448
  591.9 179.6 %all-reduce.7.cloned.1.call-done = f32[4352,1088]{0,1:T(8,128)} async-done(((f32[4352,1088]{0,1:T(8,128)}), f32[4352,1088]{0,1:T(8,128)}) %all-reduce.7.cloned.1.call-update) | async-done | bytes 18939920
  774.5 217.9 %reduce-scatter.20.cloned.1.call-done = f32[136,1088]{1,0:T(8,128)} async-done(((f32[4352,1088]{1,0:T(8,128)}), f32[136,1088]{1,0:T(8,128)}) %reduce-scatter.20.cloned.1.call-update) | async-done | bytes 591888
  992.4 221.2 %reduce-scatter.18.cloned.1.call-done = f32[136,1088]{1,0:T(8,128)} async-done(((f32[4352,1088]{1,0:T(8,128)}), f32[136,1088]{1,0:T(8,128)}) %reduce-scatter.18.cloned.1.call-update) | async-done | bytes 591888
  (288 shorter events, 114.8 us)
Async XLA Ops:
  7.2 91.9 %all-gather.6.cloned.1.call-start = ((), (), s32[]{:S(2)}) async-start(), calls=%async_computation.4 | async-start | bytes 10340352 | tf_op jit(solution)/shard_map/all_gather | solution.py:254
  7.9 119.9 %all-gather.8.cloned.1.call-start = ((), (), s32[]{:S(2)}) async-start(), calls=%async_computation.5 | async-start | bytes 2785280 | tf_op jit(solution)/shard_map/all_gather | solution.py:79
  53.7 50.9 %copy-start.49 = (f32[128]{0:T(128)}, f32[128]{0:T(128)S(1)}, u32[]{:S(2)}) copy-start(f32[128]{0:T(128)S(1)} %get-tuple-element.104) | copy-start | bytes 1540
  54.9 49.7 %copy-start.73 = (f32[128]{0:T(128)}, f32[128]{0:T(128)S(1)}, u32[]{:S(2)}) copy-start(f32[128]{0:T(128)S(1)} %get-tuple-element.36) | copy-start | bytes 1540
  54.9 50.6 %copy-start.71 = (f32[128]{0:T(128)}, f32[128]{0:T(128)S(1)}, u32[]{:S(2)}) copy-start(f32[128]{0:T(128)S(1)} %get-tuple-element.37) | copy-start | bytes 1540
  54.9 49.7 %copy-start.62 = (f32[128]{0:T(128)}, f32[128]{0:T(128)S(1)}, u32[]{:S(2)}) copy-start(f32[128]{0:T(128)S(1)} %fusion.143) | copy-start | bytes 1540
  105.5 48.1 %all-gather.14.cloned.1.call-start = ((), (), s32[]{:S(2)}) async-start(), calls=%async_computation.8 | async-start | bytes 2785280 | tf_op jit(solution)/shard_map/all_gather | solution.py:79
  112.0 129.1 %all-gather.10.cloned.1.call-start = ((), (), s32[]{:S(2)}) async-start(), calls=%async_computation.6 | async-start | bytes 10340352 | tf_op jit(solution)/shard_map/all_gather | solution.py:255
  112.6 214.6 %all-gather.12.cloned.1.call-start = ((), (), s32[]{:S(2)}) async-start(), calls=%async_computation.7 | async-start | bytes 10340352 | tf_op jit(solution)/shard_map/all_gather | solution.py:256
  113.1 286.4 %reduce-scatter.16.cloned.1.call-start = ((), (), s32[]{:S(2)}) async-start(), calls=%async_computation.10 | async-start | bytes 2785280
  138.1 214.4 %copy-start.51 = (f32[128]{0:T(128)}, f32[128]{0:T(128)S(1)}, u32[]{:S(2)}) copy-start(f32[128]{0:T(128)S(1)} %broadcast_multiply_fusion.2) | copy-start | bytes 1540
  163.5 77.6 %copy-start.6 = (f32[128,1088]{0,1:T(8,128)}, f32[128,1088]{0,1:T(8,128)S(1)}, u32[]{:S(2)}) copy-start(f32[128,1088]{0,1:T(8,128)S(1)} %get-tuple-element.88) | copy-start | bytes 1671172
  163.6 188.9 %copy-start.53 = (f32[128]{0:T(128)}, f32[128]{0:T(128)S(1)}, u32[]{:S(2)}) copy-start(f32[128]{0:T(128)S(1)} %broadcast_multiply_fusion) | copy-start | bytes 1540
  163.8 188.7 %copy-start.57 = (f32[128]{0:T(128)}, f32[128]{0:T(128)S(1)}, u32[]{:S(2)}) copy-start(f32[128]{0:T(128)S(1)} %fusion.144) | copy-start | bytes 1540
  163.8 188.7 %copy-start.60 = (f32[128]{0:T(128)}, f32[128]{0:T(128)S(1)}, u32[]{:S(2)}) copy-start(f32[128]{0:T(128)S(1)} %fusion.146) | copy-start | bytes 1540
  368.6 66.0 %reduce-scatter.14.cloned.1.call-start = ((), (), s32[]{:S(2)}) async-start(), calls=%async_computation.9 | async-start | bytes 2785280
  382.3 389.2 %all-reduce.7.cloned.1.call-start = ((), (), s32[]{:S(2)}) async-start(), calls=%async_computation.11 | async-start | bytes 37879808
  465.0 527.4 %reduce-scatter.20.cloned.1.call-start = ((), (), s32[]{:S(2)}) async-start(), calls=%async_computation.13 | async-start | bytes 20680704
  491.2 722.4 %reduce-scatter.18.cloned.1.call-start = ((), (), s32[]{:S(2)}) async-start(), calls=%async_computation.12 | async-start | bytes 20680704
  546.4 42.9 %copy-start.19 = (f32[128,1088]{0,1:T(8,128)S(1)}, f32[128,1088]{0,1:T(8,128)}, u32[]{:S(2)}) copy-start(f32[128,1088]{0,1:T(8,128)} %copy-done.18) | copy-start | bytes 1671172
  546.4 42.9 %copy-start.21 = (f32[128,1088]{0,1:T(8,128)S(1)}, f32[128,1088]{0,1:T(8,128)}, u32[]{:S(2)}) copy-start(f32[128,1088]{0,1:T(8,128)} %copy-done.20) | copy-start | bytes 1671172
  546.4 42.9 %copy-start.26 = (bf16[2,128,1088]{1,2,0:T(8,128)(2,1)S(1)}, bf16[2,128,1088]{1,2,0:T(8,128)(2,1)}, u32[]{:S(2)}) copy-start(bf16[2,128,1088]{1,2,0:T(8,128)(2,1)} %param.8) | copy-start | bytes 1671172
  546.4 42.9 %copy-start.68 = (f32[128]{0:T(128)S(1)}, f32[128]{0:T(128)}, u32[]{:S(2)}) copy-start(f32[128]{0:T(128)} %copy-done.67) | copy-start | bytes 1540
  546.4 42.9 %copy-start.70 = (f32[128]{0:T(128)S(1)}, f32[128]{0:T(128)}, u32[]{:S(2)}) copy-start(f32[128]{0:T(128)} %copy-done.69) | copy-start | bytes 1540
  (73 other events, 504.2 us)
Sparse Core Ops, SparseCore 0:
  10.9 88.0 all-gather.5
  105.6 22.1 all-gather.7
  129.9 23.5 all-gather.13
  156.4 84.7 all-gather.9
  243.9 83.2 all-gather.11
  368.7 30.7 reduce-scatter.15
  402.2 32.3 reduce-scatter.13
  465.1 306.4 all-reduce.6
  778.6 213.7 reduce-scatter.19
  1000.4 213.1 reduce-scatter.17
where the time goes:
time: 1230 us; the launch traced here: 1220 us
  waiting for transfers between devices  874 us (71%)
  matrix products  183 us (15%)
  blocking collectives  83.7 us (7%)
  other arithmetic  36.1 us (3%)
  local copies, waits for them, and re-layouts  27.3 us (2%)
  between operations  15.6 us (1%)
    unnamed x15, waiting for transfers between devices  650 us
    unnamed x2, blocking collectives  83.7 us
    dot_general x8, matrix products, contract_rows(): lax.dot_general(left, right, (((0,), (0,)), ((), ())), preferred_element_...  80.1 us
    all_gather x1, waiting for transfers between devices, shards(): lax.all_gather(w_up, ('dp', 'ctx'), axis=1, tiled=True)  77.3 us
    all_gather x1, waiting for transfers between devices, shards(): lax.all_gather(w_down, ('dp', 'ctx'), axis=0, tiled=True)  72.8 us
    all_gather x1, waiting for transfers between devices, shards(): lax.all_gather(w_attn, ('dp', 'ctx'), axis=1, tiled=True)  44.1 us
    dot_general x8, matrix products, contract_cols(): lax.dot_general(left, right, (((1,), (1,)), ((), ())), preferred_element_...  37.6 us
    all_gather x2, waiting for transfers between devices, attend_forward(): lax.all_gather(key_values, 'ctx', axis=0, tiled=True)  29.2 us
  transfers between devices with their start and end apart: 10, of which 10 were waited for; matrix products, arithmetic and copies ran while one was open for 14% of the time, Pallas kernels for 0%

commit v1 on v0

v1 whole, which is shorter than its diff:
```python
import jax
import jax.numpy as jnp
from jax import lax
from jax.sharding import PartitionSpec as P

HEAD_DIM = 64
HALO = 32
NEG_FILL = -1e30
EPSILON = 1e-05
BF = jnp.bfloat16
F32 = jnp.float32
BOTH = ("dp", "ctx")
CORE_PAIRS = [(0, 1), (1, 0), (2, 3), (3, 2)]
CHIP_PAIRS = [(0, 2), (2, 0), (1, 3), (3, 1)]
BLOCKS = (0, 2, 1, 3)
SIDE_PAIRS = [(p, p ^ 1) for p in range(8)]


def shift_pairs(step):
    return [(z * 2 + y, ((z + step) % 4) * 2 + y) for z in range(4) for y in range(2)]


def dot(left, right, left_dim, right_dim):
    return lax.dot_general(
        left, right, (((left_dim,), (right_dim,)), ((), ())), preferred_element_type=F32
    )


def norm_stats(values):
    centred = values - jnp.mean(values, axis=-1, keepdims=True)
    scale = lax.rsqrt(jnp.mean(centred * centred, axis=-1, keepdims=True) + EPSILON)
    return centred * scale, scale


def norm_pull(grad, hat, scale, gain):
    grad_hat = grad * gain
    along = jnp.mean(grad_hat * hat, axis=-1, keepdims=True)
    return scale * (grad_hat - jnp.mean(grad_hat, axis=-1, keepdims=True) - hat * along)


def row_gather(mine):
    across = lax.ppermute(mine, "ctx", CHIP_PAIRS)
    pair = jnp.concatenate([mine, across], axis=1)
    return jnp.concatenate([pair, lax.ppermute(pair, "ctx", CORE_PAIRS)], axis=1)


def row_scatter(partial):
    half = partial.shape[1] // 2
    rows = half // 2
    arrived = lax.ppermute(partial[:, half:].astype(BF), "ctx", CORE_PAIRS)
    other = partial[:, rows:half].astype(F32) + arrived[:, rows:].astype(F32)
    across = lax.ppermute(other.astype(BF), "ctx", CHIP_PAIRS)
    return partial[:, :rows].astype(F32) + arrived[:, :rows].astype(F32) + across.astype(F32)


def block_gather(block):
    near = [block] + [lax.ppermute(block, "dp", shift_pairs(k)) for k in (1, 2, 3)]
    return [b for own in near for b in (own, lax.ppermute(own, "dp", SIDE_PAIRS))]


def block_scatter(blocks):
    total = None
    for k in range(4):
        arrived = lax.ppermute(blocks[2 * k + 1], "dp", SIDE_PAIRS)
        both = blocks[2 * k].astype(F32) + arrived.astype(F32)
        if k:
            back = [(b, a) for a, b in shift_pairs(k)]
            both = lax.ppermute(both.astype(BF), "dp", back).astype(F32)
        total = both if total is None else total + both
    return total


def dp_order(z, y):
    return [((z - k) % 4) * 2 + (y ^ s) for k in range(4) for s in range(2)]


def pick(stacked, index):
    return lax.dynamic_index_in_dim(stacked, index, axis=0, keepdims=False)


def reorder(table, order):
    hot = (order[:, None] == jnp.arange(table.shape[0])[None, :]).astype(F32)
    return jnp.sum(hot[:, :, None] * table[None], axis=1)


def reorder_back(table, order):
    hot = (order[:, None] == jnp.arange(table.shape[0])[None, :]).astype(F32)
    return jnp.sum(hot[:, :, None] * table[:, None, :], axis=0)


def ctx_table(mine, ctx):
    across = lax.ppermute(mine[None], "ctx", CHIP_PAIRS)
    pair = jnp.concatenate([mine[None], across], axis=0)
    table = jnp.concatenate([pair, lax.ppermute(pair, "ctx", CORE_PAIRS)], axis=0)
    return reorder_back(table.astype(F32), jnp.stack([ctx ^ j for j in BLOCKS]))


class Aligned:
    def __init__(self, w_attn):
        self.dp = lax.axis_index("dp")
        self.ctx = lax.axis_index("ctx")
        self.z, self.y = self.dp // 2, self.dp % 2
        self.order = jnp.stack(dp_order(self.z, self.y))
        self.width = w_attn.shape[1]
        self.odd = self.y == 1
        self.last = self.ctx == 3

    def attn_weights(self, w_attn, vectors):
        turned = w_attn.T
        width, model = turned.shape
        pairs = []
        for p in range(8):
            for c in range(4):
                to = (c - 1) % 4 if p % 2 else (c + 1) % 4
                pairs.append((p * 4 + c, p * 4 + to))
        edge = jnp.where(self.odd, turned[:HALO], turned[width - HALO :])
        halo = lax.ppermute(edge, BOTH, pairs)
        none = jnp.zeros_like(halo)
        wide = jnp.concatenate(
            [jnp.where(self.odd, none, halo), turned, jnp.where(self.odd, halo, none)], axis=0
        )
        odd = self.y
        body = lax.dynamic_slice_in_dim(wide, HALO - 8 * self.ctx + HALO * odd, 128, axis=0)
        extra = lax.dynamic_slice_in_dim(wide, width + HALO * odd, HALO, axis=0)
        extra = jnp.where(self.last, extra, jnp.zeros_like(extra))
        table = ctx_table(vectors, self.ctx).astype(BF).reshape(-1)
        lines = jnp.pad(table, (0, 2 * model - table.shape[0])).reshape(2, model)
        lines = jnp.pad(lines, ((0, 14), (0, 0)))
        block = jnp.concatenate([body, extra, lines], axis=0)
        got = jnp.stack(block_gather(block)).reshape(8, 176, model)
        regions, vecs = [], []
        for region in range(4):
            k = (self.z - region) % 4
            first, second = [pick(got, k * 2 + (self.y ^ side)) for side in range(2)]
            regions.append(
                jnp.concatenate(
                    [first[:128], second[:128], first[128:160], second[128:160]], axis=0
                )
            )
            vecs += [first[160:162].reshape(-1), second[160:162].reshape(-1)]
        whole = jnp.concatenate([v[: 4 * vectors.shape[0]] for v in vecs])
        return regions, whole.astype(F32)

    def attn_owned(self, parts):
        sides = []
        for part in parts:
            first = jnp.concatenate([part[:128], part[256:288]], axis=0)
            second = jnp.concatenate([part[128:256], part[288:320]], axis=0)
            sides.append((first, second))
        summed = []
        for first, second in sides:
            away = jnp.where(self.odd, first, second).astype(BF)
            keep = jnp.where(self.odd, second, first).astype(F32)
            summed.append(keep + lax.ppermute(away, "dp", SIDE_PAIRS).astype(F32))
        own = pick(jnp.stack(summed), self.z)
        table = jnp.stack([s.astype(BF) for s in summed])
        for k in (1, 2, 3):
            back = [(b, a) for a, b in shift_pairs(k)]
            own = own + lax.ppermute(pick(table, (self.z - k) % 4), "dp", back).astype(F32)
        pairs = []
        for p in range(8):
            for c in range(4):
                to = (c + 1) % 4 if p % 2 else (c - 1) % 4
                pairs.append((p * 4 + c, p * 4 + to))
        body, extra = own[:128], own[128:]
        tail = jnp.where(self.last, extra, body[128 - HALO :])
        edge = jnp.where(self.odd, tail, body[:HALO])
        halo = lax.ppermute(edge, BOTH, pairs)
        halo = jnp.where(self.last & (self.y == 0), extra, halo)
        wide = jnp.where(
            self.odd,
            jnp.concatenate([halo, body], axis=0),
            jnp.concatenate([body, halo], axis=0),
        )
        start = jnp.where(self.odd, 8 * self.ctx, 8 * self.ctx)
        return lax.dynamic_slice_in_dim(wide, start, self.width, axis=0)

    def mlp_weights(self, w_up, w_down):
        width = self.width
        blocks = block_gather(jnp.concatenate([w_up.T, w_down], axis=0))
        return (
            jnp.concatenate([b[:width] for b in blocks], axis=0),
            jnp.concatenate([b[width:] for b in blocks], axis=0),
        )

    def mlp_owned(self, up_part, down_part):
        width = self.width
        blocks = [
            jnp.concatenate(
                [up_part[i * width : (i + 1) * width], down_part[i * width : (i + 1) * width]],
                axis=0,
            )
            for i in range(8)
        ]
        owned = block_scatter(blocks)
        return owned[:width], owned[width:]

    def vector_owned(self, part):
        each = part.shape[0] // 32
        table = part.reshape(8, 4, each).transpose(1, 0, 2)
        table = jnp.stack([pick(table, self.ctx ^ j) for j in BLOCKS])
        mine = table[:2] + lax.ppermute(table[2:], "ctx", CORE_PAIRS)
        mine = mine[0] + lax.ppermute(mine[1], "ctx", CHIP_PAIRS)
        sides = mine.reshape(4, 2, each).transpose(1, 0, 2)
        mine = pick(sides, self.y) + lax.ppermute(pick(sides, 1 - self.y), "dp", SIDE_PAIRS)
        total = pick(mine, self.z)
        for k in (1, 2, 3):
            back = [(b, a) for a, b in shift_pairs(k)]
            total = total + lax.ppermute(pick(mine, (self.z - k) % 4)[None], "dp", back)[0]
        return total


class Plain:
    def __init__(self, w_attn):
        self.ctx = lax.axis_index("ctx")
        self.order = jnp.arange(lax.axis_size("dp"))
        self.width = w_attn.shape[1]
        self.last = self.ctx == lax.axis_size("ctx") - 1

    def attn_weights(self, w_attn, vectors):
        model = w_attn.shape[0]
        whole = lax.all_gather(w_attn.T, BOTH, axis=0, tiled=True)
        regions = [
            head_rows(whole[r * model : (r + 1) * model], self.ctx, self.last) for r in range(4)
        ]
        return regions, lax.all_gather(vectors, BOTH, axis=0, tiled=True).astype(F32)

    def attn_owned(self, parts):
        whole = jnp.concatenate([head_rows_back(p, self.ctx, self.last) for p in parts], axis=0)
        return lax.psum_scatter(whole.astype(BF), BOTH, scatter_dimension=0, tiled=True).astype(F32)

    def mlp_weights(self, w_up, w_down):
        return (
            lax.all_gather(w_up.T, "dp", axis=0, tiled=True),
            lax.all_gather(w_down, "dp", axis=0, tiled=True),
        )

    def mlp_owned(self, up_part, down_part):
        return tuple(
            lax.psum_scatter(p.astype(BF), "dp", scatter_dimension=0, tiled=True).astype(F32)
            for p in (up_part, down_part)
        )

    def vector_owned(self, part):
        return lax.psum_scatter(part, BOTH, scatter_dimension=0, tiled=True)


def head_rows(table, ctx, last):
    middle = 8 * HEAD_DIM
    first = lax.dynamic_slice_in_dim(table, 128 * ctx, 128, axis=0)
    second = lax.dynamic_slice_in_dim(table, middle + HEAD_DIM + 128 * ctx, 128, axis=0)
    mid = table[middle : middle + HEAD_DIM]
    return jnp.concatenate([first, second, jnp.where(last, mid, jnp.zeros_like(mid))], axis=0)


def head_rows_back(mine, ctx, last):
    middle = 8 * HEAD_DIM
    table = jnp.zeros((2 * middle + HEAD_DIM,) + mine.shape[1:], mine.dtype)
    table = lax.dynamic_update_slice_in_dim(table, mine[:128], 128 * ctx, axis=0)
    table = lax.dynamic_update_slice_in_dim(
        table, mine[128:256], middle + HEAD_DIM + 128 * ctx, axis=0
    )
    mid = jnp.where(last, mine[256:], jnp.zeros_like(mine[256:]))
    return lax.dynamic_update_slice_in_dim(table, mid, middle, axis=0)


def gelu_parts(hidden):
    factor = 0.7978845608028654
    square = hidden * hidden
    bent = jnp.tanh(factor * hidden * (1.0 + 0.044715 * square))
    active = 0.5 * hidden * (1.0 + bent)
    slope = 0.5 * (1.0 + bent) + 0.5 * hidden * (1.0 - bent * bent) * factor * (
        1.0 + 3 * 0.044715 * square
    )
    return active, slope


def split_heads(flat):
    return flat.reshape(flat.shape[:-1] + (flat.shape[-1] // HEAD_DIM, HEAD_DIM))


def masked_scores(queries, keys, allowed):
    scores = jnp.einsum("mqhd,mkhd->mhqk", queries, keys, preferred_element_type=F32)
    return jnp.where(allowed[:, None], scores * HEAD_DIM ** (-0.5), NEG_FILL)


def attend(queries, keys, values, allowed):
    scores = masked_scores(queries, keys, allowed)
    top = jnp.max(scores, axis=-1, keepdims=True)
    weights = jnp.exp(scores - top)
    total = jnp.sum(weights, axis=-1, keepdims=True)
    probs = (weights / total).astype(BF)
    heads = jnp.einsum("mhqk,mkhd->mqhd", probs, values, preferred_element_type=F32)
    return heads, top + jnp.log(total)


def attend_pull(queries, keys, values, allowed, log_total, heads, grad):
    scale = HEAD_DIM ** (-0.5)
    probs = jnp.exp(masked_scores(queries, keys, allowed) - log_total)
    delta = jnp.einsum("mqhd,mqhd->mhq", grad.astype(F32), heads)
    grad_probs = jnp.einsum("mqhd,mkhd->mhqk", grad, values, preferred_element_type=F32)
    grad_scores = (probs * (grad_probs - delta[..., None])).astype(BF)
    dq = scale * jnp.einsum("mhqk,mkhd->mqhd", grad_scores, keys, preferred_element_type=F32)
    dk = scale * jnp.einsum("mhqk,mqhd->mkhd", grad_scores, queries, preferred_element_type=F32)
    dv = jnp.einsum("mhqk,mqhd->mkhd", probs.astype(BF), grad, preferred_element_type=F32)
    return dq, dk, dv


def shards(tokens, cotangent, w_attn, w_up, w_down, vectors, segments):
    micro, rows, model = tokens.shape
    ctx = lax.axis_index("ctx")
    group = rows * 4
    flat = micro * group
    n_dp = lax.axis_size("dp")
    fits = n_dp == 8 and lax.axis_size("ctx") == 4 and w_attn.shape == (1088, 136)
    plan = (Aligned if fits else Plain)(w_attn)

    regions, vec = plan.attn_weights(w_attn, vectors)
    pieces = [vec[i * model : (i + 1) * model] for i in range(8)]
    gain_one, bias_one, q_bias, v_bias, out_bias, gain_two, bias_two, down_bias = pieces
    up_bias = vec[8 * model :].reshape(n_dp, 4, plan.width)
    up_bias = reorder(pick(up_bias.transpose(1, 0, 2), ctx), plan.order).reshape(-1)
    w_qkv = jnp.concatenate(regions[:3], axis=0)
    w_out = regions[3]
    own_width = w_out.shape[0]

    all_tokens = row_gather(tokens).reshape(flat, model)
    all_grads = row_gather(cotangent).reshape(flat, model)
    up, down = plan.mlp_weights(w_up, w_down)

    ranks = [ctx ^ j for j in BLOCKS]
    starts = segments[:, 0].reshape(micro, 4, rows).transpose(1, 0, 2)
    starts = jnp.concatenate([pick(starts, r) for r in ranks], axis=1)
    places = jnp.concatenate([r * rows + jnp.arange(rows) for r in ranks])
    allowed = (places[None, None, :] <= places[None, :, None]) & (
        starts[:, None, :] == starts[:, :, None]
    )

    hat_all, _ = norm_stats(all_tokens.astype(F32))
    normed_one = (hat_all * gain_one + bias_one).astype(BF)
    own_q = head_rows(q_bias[:, None], ctx, plan.last)[:, 0]
    own_v = head_rows(v_bias[:, None], ctx, plan.last)[:, 0]
    qkv_bias = jnp.concatenate([own_q, jnp.zeros_like(own_q), own_v])
    projected = (dot(normed_one, w_qkv, 1, 1) + qkv_bias).astype(BF)
    grouped = projected.reshape(micro, group, 3 * own_width)
    queries, keys, values = [
        split_heads(grouped[..., i * own_width : (i + 1) * own_width]) for i in range(3)
    ]
    heads, log_total = attend(queries, keys, values, allowed)
    heads_out = heads.reshape(flat, own_width).astype(BF)
    branch = dot(heads_out, w_out, 1, 0).reshape(micro, group, model)
    tokens32 = tokens.astype(F32)
    middle = tokens32 + row_scatter(branch) + out_bias

    hat_two, scale_two = norm_stats(middle)
    normed_two = row_gather((hat_two * gain_two + bias_two).astype(BF)).reshape(flat, model)
    hidden = dot(normed_two, up, 1, 1) + up_bias
    active, slope = gelu_parts(hidden)
    active = active.astype(BF)
    grad_hidden = (dot(all_grads, down, 1, 1) * slope).astype(BF)
    back_two = row_scatter(dot(grad_hidden, up, 1, 0).reshape(micro, group, model))
    feed = row_scatter(dot(active, down, 1, 0).reshape(micro, group, model))
    mixed = (middle + feed + down_bias).astype(BF)
    down_part = dot(active, all_grads, 0, 0).astype(BF)
    up_part = dot(grad_hidden, normed_two, 0, 0).astype(BF)
    up_owned, down_owned = plan.mlp_owned(up_part, down_part)
    up_bias_part = jnp.sum(grad_hidden.astype(F32), axis=0)

    grad_out = cotangent.astype(F32)
    grad_middle = grad_out + norm_pull(back_two, hat_two, scale_two, gain_two)
    own_branch = grad_middle.astype(BF)
    grad_branch = row_gather(own_branch).reshape(flat, model)
    out_part = dot(heads_out, grad_branch, 0, 0).astype(BF)
    grad_heads = dot(grad_branch, w_out, 1, 1).astype(BF).reshape(micro, group, own_width)
    pulled = attend_pull(
        queries, keys, values, allowed, log_total, heads, split_heads(grad_heads)
    )
    grad_qkv = jnp.concatenate([g.reshape(flat, own_width) for g in pulled], axis=1).astype(BF)
    back_one = row_scatter(dot(grad_qkv, w_qkv, 1, 0).reshape(micro, group, model))
    qkv_part = dot(grad_qkv, normed_one, 0, 0).astype(BF)
    attn_owned = plan.attn_owned(
        [qkv_part[i * own_width : (i + 1) * own_width] for i in range(3)] + [out_part]
    )
    qkv_bias_part = jnp.sum(grad_qkv.astype(F32), axis=0)

    hat_one, scale_one = norm_stats(tokens32)
    input_grad = (grad_middle + norm_pull(back_one, hat_one, scale_one, gain_one)).astype(BF)

    def row_sum(values):
        return jnp.sum(values, axis=(0, 1))

    def own_bias(part):
        return head_rows_back(part[:, None], ctx, plan.last)[:, 0]

    up_rows = reorder_back(up_bias_part.reshape(n_dp, plan.width), plan.order)
    mine = (jnp.arange(4) == ctx).astype(F32)
    vector_part = jnp.concatenate(
        [
            row_sum(back_one * hat_one),
            row_sum(back_one),
            own_bias(qkv_bias_part[:own_width]),
            own_bias(qkv_bias_part[2 * own_width :]),
            row_sum(own_branch.astype(F32)),
            row_sum(back_two * hat_two),
            row_sum(back_two),
            row_sum(grad_out),
            (up_rows[:, None, :] * mine[None, :, None]).reshape(-1),
        ]
    )
    vector_owned = plan.vector_owned(vector_part)
    return (mixed, input_grad, attn_owned.T, up_owned.T, down_owned, vector_owned)


def solution(mesh):
    return jax.shard_map(
        shards,
        mesh=mesh,
        in_specs=(
            P(None, BOTH, None),
            P(None, BOTH, None),
            P(None, BOTH),
            P(None, BOTH),
            P(BOTH, None),
            P(BOTH),
            P(None, "dp", None),
        ),
        out_specs=(
            P(None, BOTH, None),
            P(None, BOTH, None),
            P(None, BOTH),
            P(None, BOTH),
            P(BOTH, None),
            P(BOTH),
        ),
        check_vma=False,
    )
```

time: 1230 us -> 538 us (0.44)
  waiting for transfers between devices: 874 us -> 202 us
  matrix products: 183 us -> 73.5 us
  local copies, waits for them, and re-layouts: 27.3 us -> 114 us
  blocking collectives: 83.7 us -> 0 us
  starting transfers between devices: 1.5 us -> 67.9 us
  other arithmetic: 36.1 us -> 69.7 us
  between operations: 15.6 us -> 2.94 us
    unnamed x15 -> x0, waiting for transfers between devices: 650 us -> none
    all_gather x5 -> x0, waiting for transfers between devices: 223 us -> none  [the longest x1 77.3 us: shards(): lax.all_gather(w_up, ('dp', 'ctx'), axis=1, tiled=True)]
    ppermute x0 -> x54, waiting for transfers between devices: none -> 202 us  [the longest x6 48.6 us: block_gather(): lax.ppermute(block, 'dp', shift_pairs(k))]
    dot_general x36 -> x18, matrix products: 183 us -> 73.5 us  [the longest x12 53.2 us: dot(): lax.dot_general(left, right, (((left_dim,), (right_dim,)), ((), ())), pre...]
    unnamed x2 -> x0, blocking collectives: 83.7 us -> none
    ppermute x0 -> x54, starting transfers between devices: none -> 67.9 us  [the longest x6 21.5 us: block_gather(): lax.ppermute(block, 'dp', shift_pairs(k))]
    unnamed x182 -> x292, local copies, waits for them, and re-layouts: 19.4 us -> 53.9 us
    convert_element_type x0 -> x16, other arithmetic: none -> 18.8 us  [the longest x4 4.45 us: row_scatter(): across = lax.ppermute(other.astype(BF), 'ctx', CHIP_PAIRS)]
  transfers between devices with their start and end apart: 10 -> 54, of which waited for: 10 -> 24; matrix products, arithmetic and copies ran while one was open for 14% -> 37% of each run, Pallas kernels for 0% -> 0%
where the time goes in v1:
time: 538 us; the launch traced here: 530 us
  waiting for transfers between devices  202 us (38%)
  local copies, waits for them, and re-layouts  114 us (21%)
  matrix products  73.5 us (14%)
  other arithmetic  69.7 us (13%)
  starting transfers between devices  67.9 us (13%)
    unnamed x292, local copies, waits for them, and re-layouts  53.9 us
    dot_general x12, matrix products, dot(): lax.dot_general(left, right, (((left_dim,), (right_dim,)), ((), ())), pre...  53.2 us
    ppermute x6, waiting for transfers between devices, block_gather(): lax.ppermute(block, 'dp', shift_pairs(k))  48.6 us
    ppermute x8, waiting for transfers between devices, block_gather(): lax.ppermute(own, 'dp', SIDE_PAIRS)  30.5 us
    ppermute x3, waiting for transfers between devices, block_scatter(): both = lax.ppermute(both.astype(BF), 'dp', back).astype(F32)  26.2 us
    ppermute x3, waiting for transfers between devices, attn_owned(): lax.ppermute(pick(table, (self.z - k) % 4), 'dp', back).astype(F32)  23.5 us
    ppermute x6, starting transfers between devices, block_gather(): lax.ppermute(block, 'dp', shift_pairs(k))  21.5 us
    ppermute x4, waiting for transfers between devices, row_gather(): across = lax.ppermute(mine, 'ctx', CHIP_PAIRS)  19.2 us
  transfers between devices with their start and end apart: 54, of which 24 were waited for; matrix products, arithmetic and copies ran while one was open for 37% of the time, Pallas kernels for 0%

profile of v1, /device:TPU:0, one launch (start us, length us, event | category | flops | bytes accessed | tf_op | source)
XLA Modules:
  0.0 530.4 jit_solution(15417597161943603972)
XLA Ops:
  2.7 5.0 collective-permute-start.21
  21.2 8.7 %collective-permute-done.5 = bf16[176,1088]{1,0:T(8,128)(2,1)} collective-permute-done((bf16[176,1088]{1,0:T(8,128)(2,1)S(1)}, bf16[176,1088]{1,0:T(8,128)(2,1)}, u32[]{:S(2)}, u32[]{:S(2)}) %collective-permute-start.5) | collective-permute-done | bytes 383008 | tf_op jit(solution)/shard_map/ppermute | solution.py:58
  32.0 12.5 %collective-permute-done.6 = bf16[176,1088]{1,0:T(8,128)(2,1)S(1)} collective-permute-done((bf16[176,1088]{1,0:T(8,128)(2,1)S(1)}, bf16[176,1088]{1,0:T(8,128)(2,1)S(1)}, u32[]{:S(2)}, u32[]{:S(2)}) %collective-permute-start.6) | collective-permute-done | bytes 383008 | tf_op jit(solution)/shard_map/ppermute | solution.py:57
  44.5 15.4 %collective-permute-start.8 = (bf16[176,1088]{1,0:T(8,128)(2,1)S(1)}, bf16[176,1088]{1,0:T(8,128)(2,1)S(1)}, u32[]{:S(2)}, u32[]{:S(2)}) collective-permute-start(bf16[176,1088]{1,0:T(8,128)(2,1)S(1)} %fusion.62), channel_id=1, source_target_pairs={{0,16},{4,20},{8,24},{12,28},{16,0},{20,4},{24,8},{28,12},{1,17},{... | collective-permute-start | bytes 1148936 | tf_op jit(solution)/shard_map/ppermute | solution.py:57
  63.9 26.6 %collective-permute-done.8 = bf16[176,1088]{1,0:T(8,128)(2,1)S(1)} collective-permute-done((bf16[176,1088]{1,0:T(8,128)(2,1)S(1)}, bf16[176,1088]{1,0:T(8,128)(2,1)S(1)}, u32[]{:S(2)}, u32[]{:S(2)}) %collective-permute-start.8) | collective-permute-done | bytes 383008 | tf_op jit(solution)/shard_map/ppermute | solution.py:57
  92.1 9.5 %collective-permute-done.10 = bf16[176,1088]{1,0:T(8,128)(2,1)S(1)} collective-permute-done((bf16[176,1088]{1,0:T(8,128)(2,1)S(1)}, bf16[176,1088]{1,0:T(8,128)(2,1)S(1)}, u32[]{:S(2)}, u32[]{:S(2)}) %collective-permute-start.10) | collective-permute-done | bytes 383008 | tf_op jit(solution)/shard_map/ppermute | solution.py:57
  103.8 21.8 %collective-permute-done.11 = bf16[176,1088]{1,0:T(8,128)(2,1)S(1)} collective-permute-done((bf16[176,1088]{1,0:T(8,128)(2,1)S(1)}, bf16[176,1088]{1,0:T(8,128)(2,1)S(1)}, u32[]{:S(2)}, u32[]{:S(2)}) %collective-permute-start.11) | collective-permute-done | bytes 383008 | tf_op jit(solution)/shard_map/ppermute | solution.py:58
  151.4 6.2 %copy.55 = f32[2,512,1088]{2,1,0:T(8,128)} copy(f32[2,512,1088]{1,2,0:T(8,128)} %maximum_convert_fusion) | data formatting | bytes 8912896 | tf_op jit(solution)/shard_map/convert_element_type | solution.py:339
  200.4 9.6 %collective-permute-done.13 = bf16[2,128,1088]{1,2,0:T(8,128)(2,1)S(1)} collective-permute-done((bf16[2,128,1088]{1,2,0:T(8,128)(2,1)S(1)}, bf16[2,128,1088]{1,2,0:T(8,128)(2,1)S(1)}, u32[]{:S(2)}, u32[]{:S(2)}) %collective-permute-start.13) | collective-permute-done | bytes 557088 | tf_op jit(solution)/shard_map/ppermute | solution.py:52
  217.9 8.8 %collective-permute-done.14 = bf16[2,128,1088]{1,2,0:T(8,128)(2,1)S(1)} collective-permute-done((bf16[2,128,1088]{1,2,0:T(8,128)(2,1)S(1)}, bf16[2,128,1088]{1,2,0:T(8,128)(2,1)S(1)}, u32[]{:S(2)}, u32[]{:S(2)}) %collective-permute-start.14) | collective-permute-done | bytes 557088 | tf_op jit(solution)/shard_map/ppermute | solution.py:42
  246.9 5.7 %convolution_add_fusion = f32[1024,1088]{0,1:T(8,128)S(1)} fusion(bf16[1024,1088]{1,0:T(8,128)(2,1)} %bitcast.284, bf16[1088,1088]{1,0:T(8,128)(2,1)} %get-tuple-element.88, f32[1088]{0:T(1024)S(1)} %add.466), kind=kOutput, calls=%fused_computation.19 | convolution fusion | flops 2425421824 | bytes 9056512 | tf_op jit(solution)/shard_map/dot_general | solution.py:24
  252.6 7.5 %convert_reduce_fusion = (f32[1088]{0:T(1024)S(1)}, bf16[1024,1088]{0,1:T(8,128)(2,1)S(1)}) fusion(f32[1024,1088]{0,1:T(8,128)S(1)} %convolution_add_fusion, bf16[1024,1088]{1,0:T(8,128)(2,1)S(1)} %bitcast.282, bf16[1088,1088]{1,0:T(8,128)(2,1)} %get-tuple-element.89), kind=kOutput, calls=%fused_computation.20 | convolution fusion | flops 2446588928 | bytes 11284736 | tf_op jit(solution)/shard_map/dot_general | solution.py:24
  264.4 7.0 %fusion.109 = f32[1024,1088]{1,0:T(8,128)} fusion(bf16[1024,1088]{0,1:T(8,128)(2,1)S(1)} %get-tuple-element.144, bf16[1088,1088]{1,0:T(8,128)(2,1)} %get-tuple-element.88), kind=kOutput, calls=%fused_computation.340 | convolution fusion | flops 2424307712 | bytes 9052160 | tf_op jit(solution)/shard_map/dot_general | solution.py:24
  271.5 5.1 convolution_convert_fusion
  276.5 5.6 %fusion.93 = f32[1024,1088]{1,0:T(8,128)S(1)} fusion(bf16[1088,1088]{1,0:T(8,128)(2,1)} %get-tuple-element.89, f32[1024,1088]{0,1:T(8,128)S(1)} %convolution_add_fusion), kind=kOutput, calls=%fused_computation.326 | convolution fusion | flops 2434334720 | bytes 11280384 | tf_op jit(solution)/shard_map/dot_general | solution.py:24
  322.9 10.7 %collective-permute-done.44 = bf16[272,1088]{1,0:T(8,128)(2,1)} collective-permute-done((bf16[272,1088]{1,0:T(8,128)(2,1)}, bf16[272,1088]{1,0:T(8,128)(2,1)}, u32[]{:S(2)}, u32[]{:S(2)}) %collective-permute-start.44) | collective-permute-done | bytes 591904 | tf_op jit(solution)/shard_map/ppermute | solution.py:64
  341.2 5.4 %collective-permute-done.46 = bf16[272,1088]{1,0:T(8,128)(2,1)} collective-permute-done((bf16[272,1088]{1,0:T(8,128)(2,1)}, bf16[272,1088]{1,0:T(8,128)(2,1)}, u32[]{:S(2)}, u32[]{:S(2)}) %collective-permute-start.46) | collective-permute-done | bytes 591904 | tf_op jit(solution)/shard_map/ppermute | solution.py:64
  350.5 10.4 %collective-permute-done.29 = bf16[2,128,1088]{1,2,0:T(8,128)(2,1)S(1)} collective-permute-done((bf16[2,128,1088]{1,2,0:T(8,128)(2,1)S(1)}, bf16[2,128,1088]{1,2,0:T(8,128)(2,1)S(1)}, u32[]{:S(2)}, u32[]{:S(2)}) %collective-permute-start.29) | collective-permute-done | bytes 557088 | tf_op jit(solution)/shard_map/ppermute | solution.py:42
  362.6 26.2 %collective-permute-done.45 = bf16[272,1088]{1,0:T(8,128)(2,1)S(1)} collective-permute-done((bf16[272,1088]{1,0:T(8,128)(2,1)S(1)}, bf16[272,1088]{1,0:T(8,128)(2,1)S(1)}, u32[]{:S(2)}, u32[]{:S(2)}) %collective-permute-start.45) | collective-permute-done | bytes 591904 | tf_op jit(solution)/shard_map/ppermute | solution.py:68
  408.3 7.1 %fusion.23 = bf16[2,512,5,64]{1,3,2,0:T(8,128)(2,1)S(1)} fusion(f32[2,5,512,512]{2,3,1,0:T(8,128)} %copy-done, f32[2,5,512]{2,1,0:T(8,128)S(1)} %copy-done.107, pred[2,512,512]{1,2,0:T(8,128)(4,1)} %copy-done.14, bf16[2,512,5,64]{1,0,3,2:T(2,128)(2,1)} %reshape_reshape.3), kind=kOutput, calls=%fused_computation.59 | convolution fusion | flops 346357760 | bytes 12341248 | tf_op jit(solution)/shard_map/mhqk,mqhd->mkhd/dot_general | solution.py:305
  452.8 5.4 %collective-permute-done.33 = bf16[160,1088]{1,0:T(8,128)(2,1)} collective-permute-done((bf16[160,1088]{1,0:T(8,128)(2,1)}, bf16[160,1088]{1,0:T(8,128)(2,1)}, u32[]{:S(2)}, u32[]{:S(2)}) %collective-permute-start.33) | collective-permute-done | bytes 348192 | tf_op jit(solution)/shard_map/ppermute | solution.py:154
  460.2 5.9 %collective-permute-done.34 = bf16[160,1088]{1,0:T(8,128)(2,1)} collective-permute-done((bf16[160,1088]{1,0:T(8,128)(2,1)}, bf16[160,1088]{1,0:T(8,128)(2,1)}, u32[]{:S(2)}, u32[]{:S(2)}) %collective-permute-start.34) | collective-permute-done | bytes 348192 | tf_op jit(solution)/shard_map/ppermute | solution.py:154
  490.1 11.2 %collective-permute-done.39 = bf16[160,1088]{1,0:T(8,128)(2,1)} collective-permute-done((bf16[160,1088]{1,0:T(8,128)(2,1)}, bf16[160,1088]{1,0:T(8,128)(2,1)}, u32[]{:S(2)}, u32[]{:S(2)}) %collective-permute-start.39) | collective-permute-done | bytes 348192 | tf_op jit(solution)/shard_map/ppermute | solution.py:159
  501.3 12.4 %collective-permute-done.38 = bf16[160,1088]{1,0:T(8,128)(2,1)} collective-permute-done((bf16[160,1088]{1,0:T(8,128)(2,1)}, bf16[160,1088]{1,0:T(8,128)(2,1)}, u32[]{:S(2)}, u32[]{:S(2)}) %collective-permute-start.38) | collective-permute-done | bytes 348192 | tf_op jit(solution)/shard_map/ppermute | solution.py:159
  (574 shorter events, 277.9 us)
Async XLA Ops:
  2.7 140.9 %collective-permute-start.21 = (bf16[272,1088]{1,0:T(8,128)(2,1)}, bf16[272,1088]{1,0:T(8,128)(2,1)}, u32[]{:S(2)}, u32[]{:S(2)}) collective-permute-start(bf16[272,1088]{1,0:T(8,128)(2,1)} %pad_maximum_fusion.9), channel_id=1, source_target_pairs={{0,24},{4,28},{8,0},{12,4},{16,8},{20,12},{24,16},{28,20},{1,25},{... | collective-permute-start | bytes 1775624 | tf_op jit(solution)/shard_map/ppermute | solution.py:57
  7.8 136.4 %collective-permute-start.19 = (bf16[272,1088]{1,0:T(8,128)(2,1)}, bf16[272,1088]{1,0:T(8,128)(2,1)}, u32[]{:S(2)}, u32[]{:S(2)}) collective-permute-start(bf16[272,1088]{1,0:T(8,128)(2,1)} %pad_maximum_fusion.9), channel_id=1, source_target_pairs={{0,16},{4,20},{8,24},{12,28},{16,0},{20,4},{24,8},{28,12},{1,17},{... | collective-permute-start | bytes 1775624 | tf_op jit(solution)/shard_map/ppermute | solution.py:57
  10.9 49.0 %collective-permute-start = (bf16[2,128,1088]{1,2,0:T(8,128)(2,1)}, bf16[2,128,1088]{1,2,0:T(8,128)(2,1)S(1)}, u32[]{:S(2)}, u32[]{:S(2)}) collective-permute-start(bf16[2,128,1088]{1,2,0:T(8,128)(2,1)} %param.7), channel_id=1, source_target_pairs={{0,2},{2,0},{1,3},{3,1},{4,6},{6,4},{5,7},{7,5},{8,10},{10,8},{9,1... | collective-permute-start | bytes 1671176 | tf_op jit(solution)/shard_map/ppermute | solution.py:42
  17.4 45.3 %collective-permute-start.25 = (bf16[2,128,1088]{1,2,0:T(8,128)(2,1)S(1)}, bf16[2,128,1088]{1,2,0:T(8,128)(2,1)S(1)}, u32[]{:S(2)}, u32[]{:S(2)}) collective-permute-start(bf16[2,128,1088]{1,2,0:T(8,128)(2,1)S(1)} %copy-done.5), channel_id=1, source_target_pairs={{0,2},{2,0},{1,3},{3,1},{4,6},{6,4},{5,7},{7,5},{8,10},{10,8},{9,1... | collective-permute-start | bytes 1671176 | tf_op jit(solution)/shard_map/ppermute | solution.py:42
  44.5 46.0 %collective-permute-start.8 = (bf16[176,1088]{1,0:T(8,128)(2,1)S(1)}, bf16[176,1088]{1,0:T(8,128)(2,1)S(1)}, u32[]{:S(2)}, u32[]{:S(2)}) collective-permute-start(bf16[176,1088]{1,0:T(8,128)(2,1)S(1)} %fusion.62), channel_id=1, source_target_pairs={{0,16},{4,20},{8,24},{12,28},{16,0},{20,4},{24,8},{28,12},{1,17},{... | collective-permute-start | bytes 1148936 | tf_op jit(solution)/shard_map/ppermute | solution.py:57
  60.0 30.5 %collective-permute-start.7 = (bf16[176,1088]{1,0:T(8,128)(2,1)S(1)}, bf16[176,1088]{1,0:T(8,128)(2,1)S(1)}, u32[]{:S(2)}, u32[]{:S(2)}) collective-permute-start(bf16[176,1088]{1,0:T(8,128)(2,1)S(1)} %collective-permute-done.6), channel_id=1, source_target_pairs={{0,4},{4,0},{8,12},{12,8},{16,20},{20,16},{24,28},{28,24},{1,5},{5... | collective-permute-start | bytes 1148936 | tf_op jit(solution)/shard_map/ppermute | solution.py:58
  62.7 83.0 %collective-permute-start.17 = (bf16[272,1088]{1,0:T(8,128)(2,1)}, bf16[272,1088]{1,0:T(8,128)(2,1)}, u32[]{:S(2)}, u32[]{:S(2)}) collective-permute-start(bf16[272,1088]{1,0:T(8,128)(2,1)} %pad_maximum_fusion.9), channel_id=1, source_target_pairs={{0,8},{4,12},{8,16},{12,20},{16,24},{20,28},{24,0},{28,4},{1,9},{5... | collective-permute-start | bytes 1775624 | tf_op jit(solution)/shard_map/ppermute | solution.py:57
  101.6 86.8 %collective-permute-start.16 = (bf16[272,1088]{1,0:T(8,128)(2,1)}, bf16[272,1088]{1,0:T(8,128)(2,1)}, u32[]{:S(2)}, u32[]{:S(2)}) collective-permute-start(bf16[272,1088]{1,0:T(8,128)(2,1)} %pad_maximum_fusion.9), channel_id=1, source_target_pairs={{0,4},{4,0},{8,12},{12,8},{16,20},{20,16},{24,28},{28,24},{1,5},{5... | collective-permute-start | bytes 1775624 | tf_op jit(solution)/shard_map/ppermute | solution.py:58
  143.6 86.9 %collective-permute-start.26 = (bf16[2,256,1088]{1,2,0:T(8,128)(2,1)}, bf16[2,256,1088]{1,2,0:T(8,128)(2,1)}, u32[]{:S(2)}, u32[]{:S(2)}) collective-permute-start(bf16[2,256,1088]{1,2,0:T(8,128)(2,1)} %pad_maximum_fusion.6), channel_id=1, source_target_pairs={{0,1},{1,0},{2,3},{3,2},{4,5},{5,4},{6,7},{7,6},{8,9},{9,8},{10,11... | collective-permute-start | bytes 3342344 | tf_op jit(solution)/shard_map/ppermute | solution.py:44
  144.1 83.8 %collective-permute-start.22 = (bf16[272,1088]{1,0:T(8,128)(2,1)}, bf16[272,1088]{1,0:T(8,128)(2,1)}, u32[]{:S(2)}, u32[]{:S(2)}) collective-permute-start(bf16[272,1088]{1,0:T(8,128)(2,1)} %collective-permute-done.21), channel_id=1, source_target_pairs={{0,4},{4,0},{8,12},{12,8},{16,20},{20,16},{24,28},{28,24},{1,5},{5... | collective-permute-start | bytes 1775624 | tf_op jit(solution)/shard_map/ppermute | solution.py:58
  145.7 68.3 %collective-permute-start.20 = (bf16[272,1088]{1,0:T(8,128)(2,1)}, bf16[272,1088]{1,0:T(8,128)(2,1)}, u32[]{:S(2)}, u32[]{:S(2)}) collective-permute-start(bf16[272,1088]{1,0:T(8,128)(2,1)} %collective-permute-done.19), channel_id=1, source_target_pairs={{0,4},{4,0},{8,12},{12,8},{16,20},{20,16},{24,28},{28,24},{1,5},{5... | collective-permute-start | bytes 1775624 | tf_op jit(solution)/shard_map/ppermute | solution.py:58
  146.2 50.3 %collective-permute-start.18 = (bf16[272,1088]{1,0:T(8,128)(2,1)}, bf16[272,1088]{1,0:T(8,128)(2,1)}, u32[]{:S(2)}, u32[]{:S(2)}) collective-permute-start(bf16[272,1088]{1,0:T(8,128)(2,1)} %collective-permute-done.17), channel_id=1, source_target_pairs={{0,4},{4,0},{8,12},{12,8},{16,20},{20,16},{24,28},{28,24},{1,5},{5... | collective-permute-start | bytes 1775624 | tf_op jit(solution)/shard_map/ppermute | solution.py:58
  289.5 73.0 %collective-permute-start.41 = (bf16[272,1088]{1,0:T(8,128)(2,1)}, bf16[272,1088]{1,0:T(8,128)(2,1)}, u32[]{:S(2)}, u32[]{:S(2)}) collective-permute-start(bf16[272,1088]{1,0:T(8,128)(2,1)} %pad_maximum_fusion.10), channel_id=1, source_target_pairs={{0,4},{4,0},{8,12},{12,8},{16,20},{20,16},{24,28},{28,24},{1,5},{5... | collective-permute-start | bytes 1775624 | tf_op jit(solution)/shard_map/ppermute | solution.py:64
  300.8 32.8 %collective-permute-start.44 = (bf16[272,1088]{1,0:T(8,128)(2,1)}, bf16[272,1088]{1,0:T(8,128)(2,1)}, u32[]{:S(2)}, u32[]{:S(2)}) collective-permute-start(bf16[272,1088]{1,0:T(8,128)(2,1)} %pad_maximum_fusion.12), channel_id=1, source_target_pairs={{0,4},{4,0},{8,12},{12,8},{16,20},{20,16},{24,28},{28,24},{1,5},{5... | collective-permute-start | bytes 1775624 | tf_op jit(solution)/shard_map/ppermute | solution.py:64
  305.4 41.3 %collective-permute-start.46 = (bf16[272,1088]{1,0:T(8,128)(2,1)}, bf16[272,1088]{1,0:T(8,128)(2,1)}, u32[]{:S(2)}, u32[]{:S(2)}) collective-permute-start(bf16[272,1088]{1,0:T(8,128)(2,1)} %pad_maximum_fusion.13), channel_id=1, source_target_pairs={{0,4},{4,0},{8,12},{12,8},{16,20},{20,16},{24,28},{28,24},{1,5},{5... | collective-permute-start | bytes 1775624 | tf_op jit(solution)/shard_map/ppermute | solution.py:64
  316.6 32.8 %collective-permute-start.23 = (bf16[2,256,1088]{1,2,0:T(8,128)(2,1)}, bf16[2,256,1088]{1,2,0:T(8,128)(2,1)S(1)}, u32[]{:S(2)}, u32[]{:S(2)}) collective-permute-start(bf16[2,256,1088]{1,2,0:T(8,128)(2,1)} %copy.110), channel_id=1, source_target_pairs={{0,1},{1,0},{2,3},{3,2},{4,5},{5,4},{6,7},{7,6},{8,9},{9,8},{10,11... | collective-permute-start | bytes 3342344 | tf_op jit(solution)/shard_map/ppermute | solution.py:50
  333.6 29.0 %collective-permute-start.43 = (bf16[272,1088]{1,0:T(8,128)(2,1)S(1)}, bf16[272,1088]{1,0:T(8,128)(2,1)S(1)}, u32[]{:S(2)}, u32[]{:S(2)}) collective-permute-start(bf16[272,1088]{1,0:T(8,128)(2,1)S(1)} %add_convert_fusion.3), channel_id=1, source_target_pairs={{8,0},{12,4},{16,8},{20,12},{24,16},{28,20},{0,24},{4,28},{9,1},{1... | collective-permute-start | bytes 1775624 | tf_op jit(solution)/shard_map/ppermute | solution.py:68
  337.5 51.4 %collective-permute-start.45 = (bf16[272,1088]{1,0:T(8,128)(2,1)S(1)}, bf16[272,1088]{1,0:T(8,128)(2,1)S(1)}, u32[]{:S(2)}, u32[]{:S(2)}) collective-permute-start(bf16[272,1088]{1,0:T(8,128)(2,1)S(1)} %add_convert_fusion.2), channel_id=1, source_target_pairs={{16,0},{20,4},{24,8},{28,12},{0,16},{4,20},{8,24},{12,28},{17,1},{... | collective-permute-start | bytes 1775624 | tf_op jit(solution)/shard_map/ppermute | solution.py:68
  349.4 39.4 %collective-permute-start.47 = (bf16[272,1088]{1,0:T(8,128)(2,1)S(1)}, bf16[272,1088]{1,0:T(8,128)(2,1)S(1)}, u32[]{:S(2)}, u32[]{:S(2)}) collective-permute-start(bf16[272,1088]{1,0:T(8,128)(2,1)S(1)} %add_convert_fusion.1), channel_id=1, source_target_pairs={{24,0},{28,4},{0,8},{4,12},{8,16},{12,20},{16,24},{20,28},{25,1},{... | collective-permute-start | bytes 1775624 | tf_op jit(solution)/shard_map/ppermute | solution.py:68
  360.9 125.6 %collective-permute-start.24 = (bf16[2,128,1088]{1,2,0:T(8,128)(2,1)}, bf16[2,128,1088]{1,2,0:T(8,128)(2,1)}, u32[]{:S(2)}, u32[]{:S(2)}) collective-permute-start(bf16[2,128,1088]{1,2,0:T(8,128)(2,1)} %add_convert_fusion.7), channel_id=1, source_target_pairs={{0,2},{2,0},{1,3},{3,1},{4,6},{6,4},{5,7},{7,5},{8,10},{10,8},{9,1... | collective-permute-start | bytes 1671176 | tf_op jit(solution)/shard_map/ppermute | solution.py:52
  362.5 28.9 %collective-permute-start.30 = (bf16[2,256,1088]{1,2,0:T(8,128)(2,1)S(1)}, bf16[2,256,1088]{1,2,0:T(8,128)(2,1)S(1)}, u32[]{:S(2)}, u32[]{:S(2)}) collective-permute-start(bf16[2,256,1088]{1,2,0:T(8,128)(2,1)S(1)} %pad_maximum_fusion.7), channel_id=1, source_target_pairs={{0,1},{1,0},{2,3},{3,2},{4,5},{5,4},{6,7},{7,6},{8,9},{9,8},{10,11... | collective-permute-start | bytes 3342344 | tf_op jit(solution)/shard_map/ppermute | solution.py:44
  443.5 27.8 %collective-permute-start.35 = (bf16[160,1088]{1,0:T(8,128)(2,1)}, bf16[160,1088]{1,0:T(8,128)(2,1)}, u32[]{:S(2)}, u32[]{:S(2)}) collective-permute-start(bf16[160,1088]{1,0:T(8,128)(2,1)} %broadcast_select_fusion.2), channel_id=1, source_target_pairs={{0,4},{4,0},{8,12},{12,8},{16,20},{20,16},{24,28},{28,24},{1,5},{5... | collective-permute-start | bytes 1044488 | tf_op jit(solution)/shard_map/ppermute | solution.py:154
  480.2 33.5 %collective-permute-start.38 = (bf16[160,1088]{1,0:T(8,128)(2,1)}, bf16[160,1088]{1,0:T(8,128)(2,1)}, u32[]{:S(2)}, u32[]{:S(2)}) collective-permute-start(bf16[160,1088]{1,0:T(8,128)(2,1)} %get-tuple-element.71), channel_id=1, source_target_pairs={{16,0},{20,4},{24,8},{28,12},{0,16},{4,20},{8,24},{12,28},{17,1},{... | collective-permute-start | bytes 1044488 | tf_op jit(solution)/shard_map/ppermute | solution.py:159
  490.1 25.4 %collective-permute-start.48 = (f32[2,8,408]{2,1,0:T(8,128)S(1)}, f32[2,8,408]{2,1,0:T(8,128)S(1)}, u32[]{:S(2)}, u32[]{:S(2)}) collective-permute-start(f32[2,8,408]{2,1,0:T(8,128)S(1)} %pad_maximum_fusion.25), channel_id=1, source_target_pairs={{0,1},{1,0},{2,3},{3,2},{4,5},{5,4},{6,7},{7,6},{8,9},{9,8},{10,11... | collective-permute-start | bytes 78344 | tf_op jit(solution)/shard_map/ppermute | solution.py:202
  (152 other events, 1963.3 us)

commit v2 on v1

--- a/solution.py
+++ b/solution.py
@@ -1,6 +1,8 @@
 import jax
 import jax.numpy as jnp
 from jax import lax
+from jax.experimental import pallas as pl
+from jax.experimental.pallas import tpu as pltpu
 from jax.sharding import PartitionSpec as P
 
 HEAD_DIM = 64
@@ -26,6 +28,10 @@
     )
 
 
+def after(value, *others):
+    return lax.optimization_barrier((value,) + others)[0]
+
+
 def norm_stats(values):
     centred = values - jnp.mean(values, axis=-1, keepdims=True)
     scale = lax.rsqrt(jnp.mean(centred * centred, axis=-1, keepdims=True) + EPSILON)
@@ -44,13 +50,12 @@
     return jnp.concatenate([pair, lax.ppermute(pair, "ctx", CORE_PAIRS)], axis=1)
 
 
-def row_scatter(partial):
-    half = partial.shape[1] // 2
-    rows = half // 2
-    arrived = lax.ppermute(partial[:, half:].astype(BF), "ctx", CORE_PAIRS)
-    other = partial[:, rows:half].astype(F32) + arrived[:, rows:].astype(F32)
+def row_scatter(keep, send):
+    rows = keep.shape[1] // 2
+    arrived = lax.ppermute(send, "ctx", CORE_PAIRS)
+    other = keep[:, rows:] + arrived[:, rows:].astype(F32)
     across = lax.ppermute(other.astype(BF), "ctx", CHIP_PAIRS)
-    return partial[:, :rows].astype(F32) + arrived[:, :rows].astype(F32) + across.astype(F32)
+    return keep[:, :rows] + arrived[:, :rows].astype(F32) + across.astype(F32)
 
 
 def block_gather(block):
@@ -127,7 +132,9 @@
         lines = jnp.pad(table, (0, 2 * model - table.shape[0])).reshape(2, model)
         lines = jnp.pad(lines, ((0, 14), (0, 0)))
         block = jnp.concatenate([body, extra, lines], axis=0)
-        got = jnp.stack(block_gather(block)).reshape(8, 176, model)
+        blocks = block_gather(block)
+        self.near = blocks[2::2]
+        got = jnp.stack(blocks)
         regions, vecs = [], []
         for region in range(4):
             k = (self.z - region) % 4
@@ -177,7 +184,8 @@
 
     def mlp_weights(self, w_up, w_down):
         width = self.width
-        blocks = block_gather(jnp.concatenate([w_up.T, w_down], axis=0))
+        block = after(jnp.concatenate([w_up.T, w_down], axis=0), *self.near)
+        blocks = block_gather(block)
         return (
             jnp.concatenate([b[:width] for b in blocks], axis=0),
             jnp.concatenate([b[width:] for b in blocks], axis=0),
@@ -275,35 +283,191 @@
     return active, slope
 
 
-def split_heads(flat):
-    return flat.reshape(flat.shape[:-1] + (flat.shape[-1] // HEAD_DIM, HEAD_DIM))
-
-
-def masked_scores(queries, keys, allowed):
-    scores = jnp.einsum("mqhd,mkhd->mhqk", queries, keys, preferred_element_type=F32)
-    return jnp.where(allowed[:, None], scores * HEAD_DIM ** (-0.5), NEG_FILL)
-
-
-def attend(queries, keys, values, allowed):
-    scores = masked_scores(queries, keys, allowed)
-    top = jnp.max(scores, axis=-1, keepdims=True)
-    weights = jnp.exp(scores - top)
-    total = jnp.sum(weights, axis=-1, keepdims=True)
-    probs = (weights / total).astype(BF)
-    heads = jnp.einsum("mhqk,mkhd->mqhd", probs, values, preferred_element_type=F32)
-    return heads, top + jnp.log(total)
-
-
-def attend_pull(queries, keys, values, allowed, log_total, heads, grad):
+def full(shape):
+    return pl.BlockSpec(shape, lambda *_: (0,) * len(shape))
+
+
+def per(shape, step=1):
+    return pl.BlockSpec((1,) + shape, lambda i: (i // step,) + (0,) * len(shape))
+
+
+def params(mib):
+    return pltpu.CompilerParams(vmem_limit_bytes=mib * 1024 * 1024)
+
+
+def attend_kernel(
+    x_ref, gain_ref, bias_ref, w_qkv_ref, qkv_bias_ref, w_out_ref, col_ref, row_ref,
+    normed_ref, qkv_ref, probs_ref, heads_ref, keep_ref, send_ref, mask_ref,
+):
+    count = probs_ref.shape[1]
+    width = count * HEAD_DIM
+    half = keep_ref.shape[1]
+    hat, _ = norm_stats(x_ref[0].astype(F32))
+    normed = (hat * gain_ref[...] + bias_ref[...]).astype(BF)
+    normed_ref[0] = normed
+    qkv_ref[0] = (dot(normed, w_qkv_ref[...], 1, 1) + qkv_bias_ref[...]).astype(BF)
+    col, row = col_ref[0], row_ref[0]
+    allowed = (row[1:2, :] <= col[:, 1:2]) & (row[0:1, :] == col[:, 0:1])
+    mask_ref[...] = jnp.where(allowed, 0.0, NEG_FILL)
+    for head in range(count):
+        lanes = slice(head * HEAD_DIM, (head + 1) * HEAD_DIM)
+        queries = qkv_ref[0, :, lanes] * jnp.asarray(HEAD_DIM ** (-0.5), BF)
+        keys = qkv_ref[0, :, width + head * HEAD_DIM : width + (head + 1) * HEAD_DIM]
+        values = qkv_ref[0, :, 2 * width + head * HEAD_DIM : 2 * width + (head + 1) * HEAD_DIM]
+        scores = dot(queries, keys, 1, 1) + mask_ref[...]
+        weights = jnp.exp(scores - jnp.max(scores, axis=1, keepdims=True))
+        probs = (weights * (1.0 / jnp.sum(weights, axis=1, keepdims=True))).astype(BF)
+        probs_ref[0, head] = probs
+        heads_ref[0, :, lanes] = dot(probs, values, 1, 0).astype(BF)
+    branch = dot(heads_ref[0], w_out_ref[...], 1, 0)
+    keep_ref[0] = branch[:half]
+    send_ref[0] = branch[half:].astype(BF)
+
+
+def attend(x, gain, bias, w_qkv, qkv_bias, w_out, col, row):
+    micro, rows, model = x.shape
+    width = w_out.shape[0]
+    count = width // HEAD_DIM
+    half = rows // 2
+    shape = jax.ShapeDtypeStruct
+    return pl.pallas_call(
+        attend_kernel,
+        grid=(micro,),
+        in_specs=[
+            per((rows, model)), full((1, model)), full((1, model)), full(w_qkv.shape),
+            full(qkv_bias.shape), full(w_out.shape), per(col.shape[1:]), per(row.shape[1:]),
+        ],
+        out_specs=[
+            per((rows, model)), per((rows, 3 * width)), per((count, rows, rows)),
+            per((rows, width)), per((half, model)), per((half, model)),
+        ],
+        out_shape=[
+            shape((micro, rows, model), BF), shape((micro, rows, 3 * width), BF),
+            shape((micro, count, rows, rows), BF), shape((micro, rows, width), BF),
+            shape((micro, half, model), F32), shape((micro, half, model), BF),
+        ],
+        scratch_shapes=[pltpu.VMEM((rows, rows), F32)],
+        compiler_params=params(56),
+        cost_estimate=pl.CostEstimate(
+            flops=2 * micro * rows * model * 4 * width,
+            bytes_accessed=12 * micro * rows * model,
+            transcendentals=micro * count * rows * rows,
+        ),
+        name="attend",
+    )(x, gain, bias, w_qkv, qkv_bias, w_out, col, row)
+
+
+def attend_pull_kernel(
+    grad_ref, w_out_ref, w_qkv_ref, qkv_ref, probs_ref, heads_ref,
+    grad_qkv_ref, keep_ref, send_ref,
+):
+    count = probs_ref.shape[1]
+    width = count * HEAD_DIM
+    half = keep_ref.shape[1]
     scale = HEAD_DIM ** (-0.5)
-    probs = jnp.exp(masked_scores(queries, keys, allowed) - log_total)
-    delta = jnp.einsum("mqhd,mqhd->mhq", grad.astype(F32), heads)
-    grad_probs = jnp.einsum("mqhd,mkhd->mhqk", grad, values, preferred_element_type=F32)
-    grad_scores = (probs * (grad_probs - delta[..., None])).astype(BF)
-    dq = scale * jnp.einsum("mhqk,mkhd->mqhd", grad_scores, keys, preferred_element_type=F32)
-    dk = scale * jnp.einsum("mhqk,mqhd->mkhd", grad_scores, queries, preferred_element_type=F32)
-    dv = jnp.einsum("mhqk,mqhd->mkhd", probs.astype(BF), grad, preferred_element_type=F32)
-    return dq, dk, dv
+    grad_heads = dot(grad_ref[0], w_out_ref[...], 1, 1).astype(BF)
+    for head in range(count):
+        lanes = [slice(i * width + head * HEAD_DIM, i * width + (head + 1) * HEAD_DIM) for i in range(3)]
+        queries, keys, values = [qkv_ref[0, :, part] for part in lanes]
+        probs = probs_ref[0, head]
+        grad = grad_heads[:, lanes[0]]
+        delta = jnp.sum(
+            grad.astype(F32) * heads_ref[0, :, lanes[0]].astype(F32), axis=1, keepdims=True
+        )
+        grad_scores = (probs.astype(F32) * (dot(grad, values, 1, 1) - delta)).astype(BF)
+        grad_qkv_ref[0, :, lanes[0]] = (scale * dot(grad_scores, keys, 1, 0)).astype(BF)
+        grad_qkv_ref[0, :, lanes[1]] = (scale * dot(grad_scores, queries, 0, 0)).astype(BF)
+        grad_qkv_ref[0, :, lanes[2]] = dot(probs, grad, 0, 0).astype(BF)
+    back = dot(grad_qkv_ref[0], w_qkv_ref[...], 1, 0)
+    keep_ref[0] = back[:half]
+    send_ref[0] = back[half:].astype(BF)
+
+
+def attend_pull(grad, w_out, w_qkv, qkv, probs, heads):
+    micro, rows, model = grad.shape
+    width = w_out.shape[0]
+    count = width // HEAD_DIM
+    half = rows // 2
+    shape = jax.ShapeDtypeStruct
+    return pl.pallas_call(
+        attend_pull_kernel,
+        grid=(micro,),
+        in_specs=[
+            per((rows, model)), full(w_out.shape), full(w_qkv.shape), per((rows, 3 * width)),
+            per((count, rows, rows)), per((rows, width)),
+        ],
+        out_specs=[per((rows, 3 * width)), per((half, model)), per((half, model))],
+        out_shape=[
+            shape((micro, rows, 3 * width), BF),
+            shape((micro, half, model), F32), shape((micro, half, model), BF),
+        ],
+        compiler_params=params(56),
+        cost_estimate=pl.CostEstimate(
+            flops=2 * micro * rows * model * 6 * width,
+            bytes_accessed=12 * micro * rows * model,
+            transcendentals=0,
+        ),
+        name="attend_pull",
+    )(grad, w_out, w_qkv, qkv, probs, heads)
+
+
+def feed_kernel(
+    x_ref, grad_ref, up_ref, down_ref, bias_ref,
+    active_ref, grad_hidden_ref, feed_keep_ref, feed_send_ref, back_keep_ref, back_send_ref, sum_ref,
+):
+    step = pl.program_id(0)
+    active, slope = gelu_parts(dot(x_ref[0], up_ref[...], 1, 1) + bias_ref[...])
+    active = active.astype(BF)
+    active_ref[0] = active
+    grad_hidden = (dot(grad_ref[0], down_ref[...], 1, 1) * slope).astype(BF)
+    grad_hidden_ref[0] = grad_hidden
+    sums = jnp.sum(grad_hidden.astype(F32), axis=0, keepdims=True)
+    back = dot(grad_hidden, up_ref[...], 1, 0)
+    feed = dot(active, down_ref[...], 1, 0)
+
+    @pl.when(step == 0)
+    def _():
+        sum_ref[...] = sums
+
+    @pl.when(step > 0)
+    def _():
+        sum_ref[...] += sums
+
+    @pl.when(step % 2 == 0)
+    def _():
+        feed_keep_ref[0] = feed
+        back_keep_ref[0] = back
+
+    @pl.when(step % 2 == 1)
+    def _():
+        feed_send_ref[0] = feed.astype(BF)
+        back_send_ref[0] = back.astype(BF)
+
+
+def feed_forward(x, grad, up, down, bias):
+    steps, half, model = x.shape
+    hidden = up.shape[0]
+    shape = jax.ShapeDtypeStruct
+    kept = shape((steps // 2, half, model), F32)
+    sent = shape((steps // 2, half, model), BF)
+    return pl.pallas_call(
+        feed_kernel,
+        grid=(steps,),
+        in_specs=[
+            per((half, model)), per((half, model)), full(up.shape), full(down.shape),
+            full(bias.shape),
+        ],
+        out_specs=[per((half, hidden))] * 2 + [per((half, model), 2)] * 4 + [full((1, hidden))],
+        out_shape=[shape((steps, half, hidden), BF)] * 2
+        + [kept, sent, kept, sent, shape((1, hidden), F32)],
+        compiler_params=params(56),
+        cost_estimate=pl.CostEstimate(
+            flops=8 * steps * half * model * hidden,
+            bytes_accessed=16 * steps * half * model,
+            transcendentals=steps * half * hidden,
+        ),
+        name="feed_forward",
+    )(x, grad, up, down, bias)
 
 
 def shards(tokens, cotangent, w_attn, w_up, w_down, vectors, segments):
@@ -324,60 +488,53 @@
     w_out = regions[3]
     own_width = w_out.shape[0]
 
-    all_tokens = row_gather(tokens).reshape(flat, model)
-    all_grads = row_gather(cotangent).reshape(flat, model)
+    all_tokens = row_gather(tokens)
+    all_grads = row_gather(after(cotangent, all_tokens))
     up, down = plan.mlp_weights(w_up, w_down)
 
     ranks = [ctx ^ j for j in BLOCKS]
     starts = segments[:, 0].reshape(micro, 4, rows).transpose(1, 0, 2)
     starts = jnp.concatenate([pick(starts, r) for r in ranks], axis=1)
-    places = jnp.concatenate([r * rows + jnp.arange(rows) for r in ranks])
-    allowed = (places[None, None, :] <= places[None, :, None]) & (
-        starts[:, None, :] == starts[:, :, None]
-    )
-
-    hat_all, _ = norm_stats(all_tokens.astype(F32))
-    normed_one = (hat_all * gain_one + bias_one).astype(BF)
+    places = jnp.concatenate([r * rows + jnp.arange(rows, dtype=jnp.int32) for r in ranks])
+    places = jnp.broadcast_to(places[None], starts.shape)
+    row_info = jnp.stack([starts, places] + [places] * 6, axis=1)
+    col_info = row_info.transpose(0, 2, 1)
+
     own_q = head_rows(q_bias[:, None], ctx, plan.last)[:, 0]
     own_v = head_rows(v_bias[:, None], ctx, plan.last)[:, 0]
     qkv_bias = jnp.concatenate([own_q, jnp.zeros_like(own_q), own_v])
-    projected = (dot(normed_one, w_qkv, 1, 1) + qkv_bias).astype(BF)
-    grouped = projected.reshape(micro, group, 3 * own_width)
-    queries, keys, values = [
-        split_heads(grouped[..., i * own_width : (i + 1) * own_width]) for i in range(3)
-    ]
-    heads, log_total = attend(queries, keys, values, allowed)
-    heads_out = heads.reshape(flat, own_width).astype(BF)
-    branch = dot(heads_out, w_out, 1, 0).reshape(micro, group, model)
+    normed_one, qkv, probs, heads, keep, send = attend(
+        all_tokens, gain_one[None], bias_one[None], w_qkv, qkv_bias[None], w_out, col_info, row_info
+    )
     tokens32 = tokens.astype(F32)
-    middle = tokens32 + row_scatter(branch) + out_bias
+    middle = tokens32 + row_scatter(keep, send) + out_bias
 
     hat_two, scale_two = norm_stats(middle)
-    normed_two = row_gather((hat_two * gain_two + bias_two).astype(BF)).reshape(flat, model)
-    hidden = dot(normed_two, up, 1, 1) + up_bias
-    active, slope = gelu_parts(hidden)
-    active = active.astype(BF)
-    grad_hidden = (dot(all_grads, down, 1, 1) * slope).astype(BF)
-    back_two = row_scatter(dot(grad_hidden, up, 1, 0).reshape(micro, group, model))
-    feed = row_scatter(dot(active, down, 1, 0).reshape(micro, group, model))
+    normed_two = row_gather((hat_two * gain_two + bias_two).astype(BF))
+    halves = (2 * micro, group // 2, model)
+    active, grad_hidden, feed_keep, feed_send, back_keep, back_send, up_bias_part = feed_forward(
+        normed_two.reshape(halves), all_grads.reshape(halves), up, down, up_bias[None]
+    )
+    back_two = row_scatter(back_keep, back_send)
+    feed = row_scatter(feed_keep, feed_send)
     mixed = (middle + feed + down_bias).astype(BF)
-    down_part = dot(active, all_grads, 0, 0).astype(BF)
-    up_part = dot(grad_hidden, normed_two, 0, 0).astype(BF)
+
+    def rows_of(values):
+        return values.reshape(flat, values.shape[-1])
+
+    down_part = dot(rows_of(active), rows_of(all_grads), 0, 0).astype(BF)
+    up_part = dot(rows_of(grad_hidden), rows_of(normed_two), 0, 0).astype(BF)
     up_owned, down_owned = plan.mlp_owned(up_part, down_part)
-    up_bias_part = jnp.sum(grad_hidden.astype(F32), axis=0)
 
     grad_out = cotangent.astype(F32)
     grad_middle = grad_out + norm_pull(back_two, hat_two, scale_two, gain_two)
     own_branch = grad_middle.astype(BF)
-    grad_branch = row_gather(own_branch).reshape(flat, model)
-    out_part = dot(heads_out, grad_branch, 0, 0).astype(BF)
-    grad_heads = dot(grad_branch, w_out, 1, 1).astype(BF).reshape(micro, group, own_width)
-    pulled = attend_pull(
-        queries, keys, values, allowed, log_total, heads, split_heads(grad_heads)
-    )
-    grad_qkv = jnp.concatenate([g.reshape(flat, own_width) for g in pulled], axis=1).astype(BF)
-    back_one = row_scatter(dot(grad_qkv, w_qkv, 1, 0).reshape(micro, group, model))
-    qkv_part = dot(grad_qkv, normed_one, 0, 0).astype(BF)
+    grad_branch = row_gather(own_branch)
+    out_part = dot(rows_of(heads), rows_of(grad_branch), 0, 0).astype(BF)
+    grad_qkv, keep, send = attend_pull(grad_branch, w_out, w_qkv, qkv, probs, heads)
+    back_one = row_scatter(keep, send)
+    grad_qkv = rows_of(grad_qkv)
+    qkv_part = dot(grad_qkv, rows_of(normed_one), 0, 0).astype(BF)
     attn_owned = plan.attn_owned(
         [qkv_part[i * own_width : (i + 1) * own_width] for i in range(3)] + [out_part]
     )

time: 538 us -> 540 us (level)
  matrix products: 73.5 us -> 12.5 us
  Pallas kernels: 0 us -> 52.9 us
  local copies, waits for them, and re-layouts: 114 us -> 132 us
  waiting for transfers between devices: 202 us -> 184 us
  starting transfers between devices: 67.9 us -> 74.2 us
  other arithmetic: 69.7 us -> 75.8 us
    pallas_call x0 -> x3, Pallas kernels: none -> 52.9 us  [the longest x1 20.9 us: feed_forward(): pl.pallas_call(feed_kernel, grid=(steps,), in_specs=[per((half, model)),...]
    dot_general x12 -> x4, matrix products: 53.2 us -> 12.5 us  [dot(): lax.dot_general(left, right, (((left_dim,), (right_dim,)), ((), ())), pre...]
    ppermute x8, waiting for transfers between devices: 30.5 us -> 61.3 us  [block_gather(): lax.ppermute(own, 'dp', SIDE_PAIRS)]
    ppermute x6, waiting for transfers between devices: 48.6 us -> 20.6 us  [block_gather(): lax.ppermute(block, 'dp', shift_pairs(k))]
    dot_general x6 -> x0, matrix products: 20.4 us -> none  [the longest x1 7.12 us: attend_pull(): jnp.einsum('mhqk,mqhd->mkhd', probs.astype(BF), grad, preferred_element_t...]
    ppermute x3, waiting for transfers between devices: 26.2 us -> 10.1 us  [block_scatter(): both = lax.ppermute(both.astype(BF), 'dp', back).astype(F32)]
    ppermute x0 -> x9, local copies, waits for them, and re-layouts: none -> 14.6 us  [the longest x4 6.67 us: row_scatter(): across = lax.ppermute(other.astype(BF), 'ctx', CHIP_PAIRS)]
    ppermute x4, waiting for transfers between devices: 18 us -> 29.5 us  [block_scatter(): arrived = lax.ppermute(blocks[2 * k + 1], 'dp', SIDE_PAIRS)]
  transfers between devices with their start and end apart: 54 -> 54, of which waited for: 24 -> 22; matrix products, arithmetic and copies ran while one was open for 37% -> 32% of each run, Pallas kernels for 0% -> 3%
where the time goes in v2:
time: 540 us; the launch traced here: 533 us
  waiting for transfers between devices  184 us (34%)
  local copies, waits for them, and re-layouts  132 us (24%)
  other arithmetic  75.8 us (14%)
  starting transfers between devices  74.2 us (14%)
  Pallas kernels  52.9 us (10%)
  matrix products  12.5 us (2%)
    ppermute x8, waiting for transfers between devices, block_gather(): lax.ppermute(own, 'dp', SIDE_PAIRS)  61.3 us
    unnamed x163, local copies, waits for them, and re-layouts  52.8 us
    ppermute x6, starting transfers between devices, block_gather(): lax.ppermute(block, 'dp', shift_pairs(k))  31.7 us
    ppermute x4, waiting for transfers between devices, block_scatter(): arrived = lax.ppermute(blocks[2 * k + 1], 'dp', SIDE_PAIRS)  29.5 us
    pallas_call x1, Pallas kernels, feed_forward(): pl.pallas_call(feed_kernel, grid=(steps,), in_specs=[per((half, model)),...  20.9 us
    ppermute x6, waiting for transfers between devices, block_gather(): lax.ppermute(block, 'dp', shift_pairs(k))  20.6 us
    ppermute x4, waiting for transfers between devices, row_gather(): across = lax.ppermute(mine, 'ctx', CHIP_PAIRS)  18.6 us
    ppermute x4, waiting for transfers between devices, attn_owned(): summed.append(keep + lax.ppermute(away, 'dp', SIDE_PAIRS).astype(F32))  18.3 us
  transfers between devices with their start and end apart: 54, of which 22 were waited for; matrix products, arithmetic and copies ran while one was open for 32% of the time, Pallas kernels for 3%

profile of v2, /device:TPU:0, one launch (start us, length us, event | category | flops | bytes accessed | tf_op | source)
XLA Modules:
  0.0 533.4 jit_solution(322979681061752044)
XLA Ops:
  23.1 19.7 %collective-permute-done.8 = bf16[176,1088]{1,0:T(8,128)(2,1)} collective-permute-done((bf16[176,1088]{1,0:T(8,128)(2,1)}, bf16[176,1088]{1,0:T(8,128)(2,1)}, u32[]{:S(2)}, u32[]{:S(2)}) %collective-permute-start.8) | collective-permute-done | bytes 383008 | tf_op jit(solution)/shard_map/ppermute | solution.py:62
  45.7 21.3 %collective-permute-start.21 = (bf16[272,1088]{1,0:T(8,128)(2,1)S(1)}, bf16[272,1088]{1,0:T(8,128)(2,1)}, u32[]{:S(2)}, u32[]{:S(2)}) collective-permute-start(bf16[272,1088]{1,0:T(8,128)(2,1)S(1)} %pad_maximum_fusion.10), channel_id=1, source_target_pairs={{0,16},{4,20},{8,24},{12,28},{16,0},{20,4},{24,8},{28,12},{1,17},{... | collective-permute-start | bytes 1775624 | tf_op jit(solution)/shard_map/ppermute | solution.py:62
  75.9 6.5 %collective-permute-done.7 = bf16[176,1088]{1,0:T(8,128)(2,1)} collective-permute-done((bf16[176,1088]{1,0:T(8,128)(2,1)}, bf16[176,1088]{1,0:T(8,128)(2,1)}, u32[]{:S(2)}, u32[]{:S(2)}) %collective-permute-start.7) | collective-permute-done | bytes 383008 | tf_op jit(solution)/shard_map/ppermute | solution.py:63
  87.0 15.6 %collective-permute-done.9 = bf16[176,1088]{1,0:T(8,128)(2,1)S(1)} collective-permute-done((bf16[176,1088]{1,0:T(8,128)(2,1)}, bf16[176,1088]{1,0:T(8,128)(2,1)S(1)}, u32[]{:S(2)}, u32[]{:S(2)}) %collective-permute-start.9) | collective-permute-done | bytes 383008 | tf_op jit(solution)/shard_map/ppermute | solution.py:63
  105.2 7.1 %collective-permute-done.11 = bf16[176,1088]{1,0:T(8,128)(2,1)S(1)} collective-permute-done((bf16[176,1088]{1,0:T(8,128)(2,1)S(1)}, bf16[176,1088]{1,0:T(8,128)(2,1)S(1)}, u32[]{:S(2)}, u32[]{:S(2)}) %collective-permute-start.11) | collective-permute-done | bytes 383008 | tf_op jit(solution)/shard_map/ppermute | solution.py:63
  143.7 15.4 %attend.1 = (bf16[2,512,1088]{2,1,0:T(8,128)(2,1)}, bf16[2,512,960]{2,1,0:T(8,128)(2,1)}, bf16[2,5,512,512]{3,2,1,0:T(8,128)(2,1)}, bf16[2,512,320]{2,1,0:T(8,12...) custom-call(bf16[2,512,1088]{2,1,0:T(8,128)(2,1)} %pad_maximum_fusion.x_ref, ...), custom_call_target="tpu_custom_call" | custom-call | flops 2852126720 | bytes 13369344 | tf_op jit(solution)/shard_map/attend/pallas_call | solution.py:333
  173.3 32.1 %collective-permute-done.20 = bf16[272,1088]{1,0:T(8,128)(2,1)} collective-permute-done((bf16[272,1088]{1,0:T(8,128)(2,1)}, bf16[272,1088]{1,0:T(8,128)(2,1)}, u32[]{:S(2)}, u32[]{:S(2)}) %collective-permute-start.20) | collective-permute-done | bytes 591904 | tf_op jit(solution)/shard_map/ppermute | solution.py:63
  216.9 8.2 %collective-permute-done.16 = bf16[2,128,1088]{1,2,0:T(8,128)(2,1)} collective-permute-done((bf16[2,128,1088]{1,2,0:T(8,128)(2,1)S(1)}, bf16[2,128,1088]{1,2,0:T(8,128)(2,1)}, u32[]{:S(2)}, u32[]{:S(2)}) %collective-permute-start.16) | collective-permute-done | bytes 557088 | tf_op jit(solution)/shard_map/ppermute | solution.py:48
  227.3 7.9 %collective-permute-done.14 = bf16[2,128,1088]{1,2,0:T(8,128)(2,1)} collective-permute-done((bf16[2,128,1088]{1,2,0:T(8,128)(2,1)S(1)}, bf16[2,128,1088]{1,2,0:T(8,128)(2,1)}, u32[]{:S(2)}, u32[]{:S(2)}) %collective-permute-start.14) | collective-permute-done | bytes 557088 | tf_op jit(solution)/shard_map/ppermute | solution.py:48
  246.8 4.2 copy.168
  254.7 4.2 copy.167
  258.9 20.9 %feed_forward.1 = (bf16[4,256,1088]{2,1,0:T(8,128)(2,1)}, bf16[4,256,1088]{2,1,0:T(8,128)(2,1)}, f32[2,256,1088]{2,1,0:T(8,128)}, bf16[2,256,1088]{2,1,0:T(8,128...) custom-call(bf16[4,256,1088]{2,1,0:T(8,128)(2,1)} %bitcast.196, ...), custom_call_target="tpu_custom_call" | custom-call | flops 9697230848 | bytes 17825792 | tf_op jit(solution)/shard_map/feed_forward/pallas_call | solution.py:453
  280.6 5.5 %convolution_convert_fusion.1 = bf16[1088,1088]{1,0:T(8,128)(2,1)S(1)} fusion(bf16[1024,1088]{1,0:T(8,128)(2,1)} %bitcast.216, bf16[1024,1088]{1,0:T(8,128)(2,1)} %bitcast.197), kind=kOutput, calls=%fused_computation.1 | convolution fusion | flops 2425491456 | bytes 6823936 | tf_op jit(solution)/shard_map/dot_general | solution.py:26
  320.9 17.5 %collective-permute-done.44 = bf16[272,1088]{1,0:T(8,128)(2,1)} collective-permute-done((bf16[272,1088]{1,0:T(8,128)(2,1)}, bf16[272,1088]{1,0:T(8,128)(2,1)}, u32[]{:S(2)}, u32[]{:S(2)}) %collective-permute-start.44) | collective-permute-done | bytes 591904 | tf_op jit(solution)/shard_map/ppermute | solution.py:69
  341.1 10.3 %collective-permute-done.46 = bf16[272,1088]{1,0:T(8,128)(2,1)} collective-permute-done((bf16[272,1088]{1,0:T(8,128)(2,1)}, bf16[272,1088]{1,0:T(8,128)(2,1)}, u32[]{:S(2)}, u32[]{:S(2)}) %collective-permute-start.46) | collective-permute-done | bytes 591904 | tf_op jit(solution)/shard_map/ppermute | solution.py:69
  385.0 10.1 %collective-permute-done.45 = bf16[272,1088]{1,0:T(8,128)(2,1)} collective-permute-done((bf16[272,1088]{1,0:T(8,128)(2,1)}, bf16[272,1088]{1,0:T(8,128)(2,1)}, u32[]{:S(2)}, u32[]{:S(2)}) %collective-permute-start.45) | collective-permute-done | bytes 591904 | tf_op jit(solution)/shard_map/ppermute | solution.py:73
  402.9 3.2 pad_maximum_fusion.1.grad_ref
  408.7 16.7 %attend_pull.1 = (bf16[2,512,960]{2,1,0:T(8,128)(2,1)}, f32[2,256,1088]{2,1,0:T(8,128)}, bf16[2,256,1088]{2,1,0:T(8,128)(2,1)}) custom-call(bf16[2,512,1088]{2,1,0:T(8,128)(2,1)} %pad_maximum_fusion.1.grad_ref, bf16[320,1088]{1,0:T(8,128)(2,1)} %pad_maximum_fusion.9.w_out_ref, bf16[960,1088]{1,0:T(8,128)(2,1)} %constant_dynamic-update-slice_fusion.w_qkv_ref, ...), custom_call_target="tpu_custom_call" | custom-call | flops 4278190080 | bytes 13369344 | tf_op jit(solution)/shard_map/attend_pull/pallas_call | solution.py:392
  450.5 5.8 %collective-permute-done.33 = bf16[160,1088]{1,0:T(8,128)(2,1)S(1)} collective-permute-done((bf16[160,1088]{1,0:T(8,128)(2,1)S(1)}, bf16[160,1088]{1,0:T(8,128)(2,1)S(1)}, u32[]{:S(2)}, u32[]{:S(2)}) %collective-permute-start.33) | collective-permute-done | bytes 348192 | tf_op jit(solution)/shard_map/ppermute | solution.py:161
  457.5 6.7 %collective-permute-done.34 = bf16[160,1088]{1,0:T(8,128)(2,1)S(1)} collective-permute-done((bf16[160,1088]{1,0:T(8,128)(2,1)S(1)}, bf16[160,1088]{1,0:T(8,128)(2,1)S(1)}, u32[]{:S(2)}, u32[]{:S(2)}) %collective-permute-start.34) | collective-permute-done | bytes 348192 | tf_op jit(solution)/shard_map/ppermute | solution.py:161
  465.3 5.8 %collective-permute-done.35 = bf16[160,1088]{1,0:T(8,128)(2,1)S(1)} collective-permute-done((bf16[160,1088]{1,0:T(8,128)(2,1)S(1)}, bf16[160,1088]{1,0:T(8,128)(2,1)S(1)}, u32[]{:S(2)}, u32[]{:S(2)}) %collective-permute-start.35) | collective-permute-done | bytes 348192 | tf_op jit(solution)/shard_map/ppermute | solution.py:161
  486.3 6.8 %collective-permute-done.32 = bf16[2,128,1088]{1,2,0:T(8,128)(2,1)} collective-permute-done((bf16[2,128,1088]{1,2,0:T(8,128)(2,1)}, bf16[2,128,1088]{1,2,0:T(8,128)(2,1)}, u32[]{:S(2)}, u32[]{:S(2)}) %collective-permute-start.32) | collective-permute-done | bytes 557088 | tf_op jit(solution)/shard_map/ppermute | solution.py:57
  502.3 12.3 %collective-permute-done.38 = bf16[160,1088]{1,0:T(8,128)(2,1)} collective-permute-done((bf16[160,1088]{1,0:T(8,128)(2,1)}, bf16[160,1088]{1,0:T(8,128)(2,1)}, u32[]{:S(2)}, u32[]{:S(2)}) %collective-permute-start.38) | collective-permute-done | bytes 348192 | tf_op jit(solution)/shard_map/ppermute | solution.py:166
  524.0 3.2 collective-permute-start.51
  (438 shorter events, 264.5 us)
Async XLA Ops:
  5.4 68.0 %collective-permute-start = (bf16[2,128,1088]{1,2,0:T(8,128)(2,1)}, bf16[2,128,1088]{1,2,0:T(8,128)(2,1)S(1)}, u32[]{:S(2)}, u32[]{:S(2)}) collective-permute-start(bf16[2,128,1088]{1,2,0:T(8,128)(2,1)} %param.7), channel_id=1, source_target_pairs={{0,2},{2,0},{1,3},{3,1},{4,6},{6,4},{5,7},{7,5},{8,10},{10,8},{9,1... | collective-permute-start | bytes 1671176 | tf_op jit(solution)/shard_map/ppermute | solution.py:48
  12.0 30.8 %collective-permute-start.8 = (bf16[176,1088]{1,0:T(8,128)(2,1)}, bf16[176,1088]{1,0:T(8,128)(2,1)}, u32[]{:S(2)}, u32[]{:S(2)}) collective-permute-start(bf16[176,1088]{1,0:T(8,128)(2,1)} %fusion.34), channel_id=1, source_target_pairs={{0,16},{4,20},{8,24},{12,28},{16,0},{20,4},{24,8},{28,12},{1,17},{... | collective-permute-start | bytes 1148936 | tf_op jit(solution)/shard_map/ppermute | solution.py:62
  14.6 28.3 %collective-permute-start.6 = (bf16[176,1088]{1,0:T(8,128)(2,1)}, bf16[176,1088]{1,0:T(8,128)(2,1)}, u32[]{:S(2)}, u32[]{:S(2)}) collective-permute-start(bf16[176,1088]{1,0:T(8,128)(2,1)} %fusion.34), channel_id=1, source_target_pairs={{0,8},{4,12},{8,16},{12,20},{16,24},{20,28},{24,0},{28,4},{1,9},{5... | collective-permute-start | bytes 1148936 | tf_op jit(solution)/shard_map/ppermute | solution.py:62
  16.1 27.5 %collective-permute-start.10 = (bf16[176,1088]{1,0:T(8,128)(2,1)}, bf16[176,1088]{1,0:T(8,128)(2,1)S(1)}, u32[]{:S(2)}, u32[]{:S(2)}) collective-permute-start(bf16[176,1088]{1,0:T(8,128)(2,1)} %fusion.34), channel_id=1, source_target_pairs={{0,24},{4,28},{8,0},{12,4},{16,8},{20,12},{24,16},{28,20},{1,25},{... | collective-permute-start | bytes 1148936 | tf_op jit(solution)/shard_map/ppermute | solution.py:62
  21.1 48.7 %collective-permute-start.5 = (bf16[176,1088]{1,0:T(8,128)(2,1)}, bf16[176,1088]{1,0:T(8,128)(2,1)S(1)}, u32[]{:S(2)}, u32[]{:S(2)}) collective-permute-start(bf16[176,1088]{1,0:T(8,128)(2,1)} %fusion.34), channel_id=1, source_target_pairs={{0,4},{4,0},{8,12},{12,8},{16,20},{20,16},{24,28},{28,24},{1,5},{5... | collective-permute-start | bytes 1148936 | tf_op jit(solution)/shard_map/ppermute | solution.py:63
  43.7 118.5 %collective-permute-start.23 = (bf16[272,1088]{1,0:T(8,128)(2,1)S(1)}, bf16[272,1088]{1,0:T(8,128)(2,1)}, u32[]{:S(2)}, u32[]{:S(2)}) collective-permute-start(bf16[272,1088]{1,0:T(8,128)(2,1)S(1)} %pad_maximum_fusion.10), channel_id=1, source_target_pairs={{0,24},{4,28},{8,0},{12,4},{16,8},{20,12},{24,16},{28,20},{1,25},{... | collective-permute-start | bytes 1775624 | tf_op jit(solution)/shard_map/ppermute | solution.py:62
  45.7 117.4 %collective-permute-start.21 = (bf16[272,1088]{1,0:T(8,128)(2,1)S(1)}, bf16[272,1088]{1,0:T(8,128)(2,1)}, u32[]{:S(2)}, u32[]{:S(2)}) collective-permute-start(bf16[272,1088]{1,0:T(8,128)(2,1)S(1)} %pad_maximum_fusion.10), channel_id=1, source_target_pairs={{0,16},{4,20},{8,24},{12,28},{16,0},{20,4},{24,8},{28,12},{1,17},{... | collective-permute-start | bytes 1775624 | tf_op jit(solution)/shard_map/ppermute | solution.py:62
  67.0 97.2 %collective-permute-start.19 = (bf16[272,1088]{1,0:T(8,128)(2,1)S(1)}, bf16[272,1088]{1,0:T(8,128)(2,1)}, u32[]{:S(2)}, u32[]{:S(2)}) collective-permute-start(bf16[272,1088]{1,0:T(8,128)(2,1)S(1)} %pad_maximum_fusion.10), channel_id=1, source_target_pairs={{0,8},{4,12},{8,16},{12,20},{16,24},{20,28},{24,0},{28,4},{1,9},{5... | collective-permute-start | bytes 1775624 | tf_op jit(solution)/shard_map/ppermute | solution.py:62
  73.4 91.7 %collective-permute-start.18 = (bf16[272,1088]{1,0:T(8,128)(2,1)S(1)}, bf16[272,1088]{1,0:T(8,128)(2,1)}, u32[]{:S(2)}, u32[]{:S(2)}) collective-permute-start(bf16[272,1088]{1,0:T(8,128)(2,1)S(1)} %pad_maximum_fusion.10), channel_id=1, source_target_pairs={{0,4},{4,0},{8,12},{12,8},{16,20},{20,16},{24,28},{28,24},{1,5},{5... | collective-permute-start | bytes 1775624 | tf_op jit(solution)/shard_map/ppermute | solution.py:63
  112.3 27.9 %collective-permute-start.1 = (bf16[2,256,1088]{1,2,0:T(8,128)(2,1)}, bf16[2,256,1088]{1,2,0:T(8,128)(2,1)}, u32[]{:S(2)}, u32[]{:S(2)}) collective-permute-start(bf16[2,256,1088]{1,2,0:T(8,128)(2,1)} %pad_maximum_fusion.7), channel_id=1, source_target_pairs={{0,1},{1,0},{2,3},{3,2},{4,5},{5,4},{6,7},{7,6},{8,9},{9,8},{10,11... | collective-permute-start | bytes 3342344 | tf_op jit(solution)/shard_map/ppermute | solution.py:50
  162.1 79.8 %collective-permute-start.24 = (bf16[272,1088]{1,0:T(8,128)(2,1)}, bf16[272,1088]{1,0:T(8,128)(2,1)}, u32[]{:S(2)}, u32[]{:S(2)}) collective-permute-start(bf16[272,1088]{1,0:T(8,128)(2,1)} %collective-permute-done.23), channel_id=1, source_target_pairs={{0,4},{4,0},{8,12},{12,8},{16,20},{20,16},{24,28},{28,24},{1,5},{5... | collective-permute-start | bytes 1775624 | tf_op jit(solution)/shard_map/ppermute | solution.py:63
  163.1 51.8 %collective-permute-start.22 = (bf16[272,1088]{1,0:T(8,128)(2,1)}, bf16[272,1088]{1,0:T(8,128)(2,1)}, u32[]{:S(2)}, u32[]{:S(2)}) collective-permute-start(bf16[272,1088]{1,0:T(8,128)(2,1)} %collective-permute-done.21), channel_id=1, source_target_pairs={{0,4},{4,0},{8,12},{12,8},{16,20},{20,16},{24,28},{28,24},{1,5},{5... | collective-permute-start | bytes 1775624 | tf_op jit(solution)/shard_map/ppermute | solution.py:63
  164.2 41.2 %collective-permute-start.20 = (bf16[272,1088]{1,0:T(8,128)(2,1)}, bf16[272,1088]{1,0:T(8,128)(2,1)}, u32[]{:S(2)}, u32[]{:S(2)}) collective-permute-start(bf16[272,1088]{1,0:T(8,128)(2,1)} %collective-permute-done.19), channel_id=1, source_target_pairs={{0,4},{4,0},{8,12},{12,8},{16,20},{20,16},{24,28},{28,24},{1,5},{5... | collective-permute-start | bytes 1775624 | tf_op jit(solution)/shard_map/ppermute | solution.py:63
  172.3 37.9 %collective-permute-start.13 = (bf16[2,128,1088]{1,2,0:T(8,128)(2,1)S(1)}, bf16[2,128,1088]{1,2,0:T(8,128)(2,1)S(1)}, u32[]{:S(2)}, u32[]{:S(2)}) collective-permute-start(bf16[2,128,1088]{1,2,0:T(8,128)(2,1)S(1)} %copy.161), channel_id=1, source_target_pairs={{0,2},{2,0},{1,3},{3,1},{4,6},{6,4},{5,7},{7,5},{8,10},{10,8},{9,1... | collective-permute-start | bytes 1671176 | tf_op jit(solution)/shard_map/ppermute | solution.py:57
  302.9 82.1 %collective-permute-start.41 = (bf16[272,1088]{1,0:T(8,128)(2,1)}, bf16[272,1088]{1,0:T(8,128)(2,1)}, u32[]{:S(2)}, u32[]{:S(2)}) collective-permute-start(bf16[272,1088]{1,0:T(8,128)(2,1)} %pad_maximum_fusion.11), channel_id=1, source_target_pairs={{0,4},{4,0},{8,12},{12,8},{16,20},{20,16},{24,28},{28,24},{1,5},{5... | collective-permute-start | bytes 1775624 | tf_op jit(solution)/shard_map/ppermute | solution.py:69
  305.8 32.5 %collective-permute-start.44 = (bf16[272,1088]{1,0:T(8,128)(2,1)}, bf16[272,1088]{1,0:T(8,128)(2,1)}, u32[]{:S(2)}, u32[]{:S(2)}) collective-permute-start(bf16[272,1088]{1,0:T(8,128)(2,1)} %pad_maximum_fusion.13), channel_id=1, source_target_pairs={{0,4},{4,0},{8,12},{12,8},{16,20},{20,16},{24,28},{28,24},{1,5},{5... | collective-permute-start | bytes 1775624 | tf_op jit(solution)/shard_map/ppermute | solution.py:69
  308.7 42.7 %collective-permute-start.46 = (bf16[272,1088]{1,0:T(8,128)(2,1)}, bf16[272,1088]{1,0:T(8,128)(2,1)}, u32[]{:S(2)}, u32[]{:S(2)}) collective-permute-start(bf16[272,1088]{1,0:T(8,128)(2,1)} %pad_maximum_fusion.14), channel_id=1, source_target_pairs={{0,4},{4,0},{8,12},{12,8},{16,20},{20,16},{24,28},{28,24},{1,5},{5... | collective-permute-start | bytes 1775624 | tf_op jit(solution)/shard_map/ppermute | solution.py:69
  311.5 52.3 %collective-permute-start.25 = (bf16[2,256,1088]{1,2,0:T(8,128)(2,1)}, bf16[2,256,1088]{1,2,0:T(8,128)(2,1)}, u32[]{:S(2)}, u32[]{:S(2)}) collective-permute-start(bf16[2,256,1088]{1,2,0:T(8,128)(2,1)} %copy.169), channel_id=1, source_target_pairs={{0,1},{1,0},{2,3},{3,2},{4,5},{5,4},{6,7},{7,6},{8,9},{9,8},{10,11... | collective-permute-start | bytes 3342344 | tf_op jit(solution)/shard_map/ppermute | solution.py:55
  313.6 71.4 %collective-permute-start.43 = (bf16[272,1088]{1,0:T(8,128)(2,1)}, bf16[272,1088]{1,0:T(8,128)(2,1)}, u32[]{:S(2)}, u32[]{:S(2)}) collective-permute-start(bf16[272,1088]{1,0:T(8,128)(2,1)} %add_convert_fusion.2), channel_id=1, source_target_pairs={{8,0},{12,4},{16,8},{20,12},{24,16},{28,20},{0,24},{4,28},{9,1},{1... | collective-permute-start | bytes 1775624 | tf_op jit(solution)/shard_map/ppermute | solution.py:73
  351.4 43.7 %collective-permute-start.45 = (bf16[272,1088]{1,0:T(8,128)(2,1)}, bf16[272,1088]{1,0:T(8,128)(2,1)}, u32[]{:S(2)}, u32[]{:S(2)}) collective-permute-start(bf16[272,1088]{1,0:T(8,128)(2,1)} %add_convert_fusion.1), channel_id=1, source_target_pairs={{16,0},{20,4},{24,8},{28,12},{0,16},{4,20},{8,24},{12,28},{17,1},{... | collective-permute-start | bytes 1775624 | tf_op jit(solution)/shard_map/ppermute | solution.py:73
  354.3 40.8 %collective-permute-start.47 = (bf16[272,1088]{1,0:T(8,128)(2,1)}, bf16[272,1088]{1,0:T(8,128)(2,1)}, u32[]{:S(2)}, u32[]{:S(2)}) collective-permute-start(bf16[272,1088]{1,0:T(8,128)(2,1)} %add_convert_fusion), channel_id=1, source_target_pairs={{24,0},{28,4},{0,8},{4,12},{8,16},{12,20},{16,24},{20,28},{25,1},{... | collective-permute-start | bytes 1775624 | tf_op jit(solution)/shard_map/ppermute | solution.py:73
  441.6 29.6 %collective-permute-start.35 = (bf16[160,1088]{1,0:T(8,128)(2,1)S(1)}, bf16[160,1088]{1,0:T(8,128)(2,1)S(1)}, u32[]{:S(2)}, u32[]{:S(2)}) collective-permute-start(bf16[160,1088]{1,0:T(8,128)(2,1)S(1)} %broadcast_select_fusion.2), channel_id=1, source_target_pairs={{0,4},{4,0},{8,12},{12,8},{16,20},{20,16},{24,28},{28,24},{1,5},{5... | collective-permute-start | bytes 1044488 | tf_op jit(solution)/shard_map/ppermute | solution.py:161
  442.7 29.6 %collective-permute-start.31 = (bf16[2,256,1088]{1,2,0:T(8,128)(2,1)S(1)}, bf16[2,256,1088]{1,2,0:T(8,128)(2,1)S(1)}, u32[]{:S(2)}, u32[]{:S(2)}) collective-permute-start(bf16[2,256,1088]{1,2,0:T(8,128)(2,1)S(1)} %copy-done.22), channel_id=1, source_target_pairs={{0,1},{1,0},{2,3},{3,2},{4,5},{5,4},{6,7},{7,6},{8,9},{9,8},{10,11... | collective-permute-start | bytes 3342344 | tf_op jit(solution)/shard_map/ppermute | solution.py:55
  484.3 30.3 %collective-permute-start.38 = (bf16[160,1088]{1,0:T(8,128)(2,1)}, bf16[160,1088]{1,0:T(8,128)(2,1)}, u32[]{:S(2)}, u32[]{:S(2)}) collective-permute-start(bf16[160,1088]{1,0:T(8,128)(2,1)} %get-tuple-element.128), channel_id=1, source_target_pairs={{16,0},{20,4},{24,8},{28,12},{0,16},{4,20},{8,24},{12,28},{17,1},{... | collective-permute-start | bytes 1044488 | tf_op jit(solution)/shard_map/ppermute | solution.py:166
  (93 other events, 1007.4 us)
